TPU v7x, 32 devices: a whole 2x2x4 slice. The times are simulated.
32 devices in a mesh: seq: 16 (over z, y, x), head: 2 (over core).
Axes of the slice: x: 2, y: 2, z: 4, core: 2. Of those that a mesh axis runs over, the one named last changes fastest.
Arguments:
- query: bfloat16 [2048, 4096], P('seq', 'head'), may hold values from -6 to 6
- keys: bfloat16 [2048, 2, 4096], P('seq', None, 'head'), may hold values from -8 to 8
- values: bfloat16 [2048, 2, 4096], P('seq', None, 'head'), may hold values from -6 to 6
- beta: float32 [2, 32, 2048], P(None, 'head', 'seq'), may hold values from 0.001 to 1
- gate_log: float32 [32, 2048], P('head', 'seq'), may hold values from -0.7 to 0
- house_count: int32 [2048], P('seq'), may hold values from 1 to 2
- out_gate: bfloat16 [2048, 4096], P('seq', 'head'), may hold values from -6 to 6
- norm_gain: float32 [128], replicated, may hold values from 0.1 to 1.9
- out_weight: bfloat16 [4096, 4096], P(None, 'head'), may hold values from -0.09375 to 0.09375
Outputs:
- mixed: bfloat16 [2048, 4096], P('seq', 'head')
All inputs are finite; a program needn't handle non-finite values.
Results may differ from a plain program's by a relative error of at most 0.0049.
Values may be sent and summed in bfloat16 or wider, within the bound.
A program may use at most 320 MiB of HBM per device.

v0:
```python
import jax
import jax.numpy as jnp
from jax import lax
from jax.sharding import PartitionSpec as P

DK = 128
DV = 128
NH = 2


epsilon = 1e-06
highest_precision = lax.Precision.HIGHEST


def shifted(shard, axis, by):
    length = lax.axis_size(axis)
    pairs = [(i, i + by) for i in range(length) if 0 <= i + by < length]
    return lax.ppermute(shard, axis, pairs)


def unit_rows(matrix):
    return matrix / jnp.sqrt(jnp.sum(matrix * matrix, axis=-1, keepdims=True) + epsilon)


def batch_stacked(einsum_form, left_side, right_hand):
    return jnp.einsum(einsum_form, left_side, right_hand, precision=highest_precision)


def stacked_product(left_side, right_hand):
    return jnp.matmul(left_side, right_hand, precision=highest_precision)


def forward_solve(lower_part, right_side):
    width = lower_part.shape[-1]
    piece = min(16, width)
    solved_rows = []
    for row_block in range(width // piece):
        first = row_block * piece
        last = first + piece
        diagonal_part = lower_part[..., first:last, first:last]
        inverse = jnp.eye(piece, dtype=jnp.float32) - diagonal_part
        power = diagonal_part
        span = 2
        while span < piece:
            power = stacked_product(power, power)
            inverse = inverse + stacked_product(inverse, power)
            span = span * 2
        target = right_side[..., first:last, :]
        if row_block > 0:
            earlier_rows = jnp.concatenate(solved_rows, axis=-2)
            target = target - stacked_product(lower_part[..., first:last, :first], earlier_rows)
        solved_rows.append(stacked_product(inverse, target))
    return jnp.concatenate(solved_rows, axis=-2)


def shards(query, keys, values, beta, gate_log, house_count, out_gate, norm_gain, out_weight):
    tok_local = query.shape[0]
    heads_here = query.shape[1] // DK
    block_tok = min(64, tok_local)
    block_count = tok_local // block_tok
    block_steps = block_tok * NH
    queries = unit_rows(query.astype(jnp.float32).reshape(tok_local, heads_here, DK))
    keyed = unit_rows(keys.astype(jnp.float32).reshape(tok_local, NH, heads_here, DK))
    valued = values.astype(jnp.float32).reshape(tok_local, NH, heads_here, DV)
    active = (jnp.arange(NH, dtype=jnp.int32)[:, None] < house_count[None, :]).astype(jnp.float32)
    strength = (
        (beta * active[:, None, :]).transpose(1, 2, 0).reshape(heads_here, block_count, block_steps)
    )
    key_blocks = keyed.transpose(2, 0, 1, 3).reshape(heads_here, block_count, block_steps, DK)
    value_blocks = valued.transpose(2, 0, 1, 3).reshape(heads_here, block_count, block_steps, DV)
    query_blocks = queries.transpose(1, 0, 2).reshape(heads_here, block_count, block_tok, DK)
    padded_log = jnp.concatenate(
        [gate_log[:, :, None], jnp.zeros((heads_here, tok_local, NH - 1), jnp.float32)], axis=2
    )
    cumulative = jnp.cumsum(padded_log.reshape(heads_here, block_count, block_steps), axis=-1)
    at_read = cumulative[..., NH - 1 :: NH]
    at_end = cumulative[..., block_steps - 1 :]
    token_positions = jnp.arange(block_steps)
    strictly = token_positions[:, None] > token_positions[None, :]
    key_gram = batch_stacked("hbmk,hbnk->hbmn", key_blocks, key_blocks)
    spread = jnp.where(strictly, cumulative[..., :, None] - cumulative[..., None, :], 0.0)
    lower_part = jnp.where(strictly, strength[..., :, None] * jnp.exp(spread) * key_gram, 0.0)
    right_side = jnp.concatenate(
        [
            (strength * jnp.exp(cumulative))[..., None] * key_blocks,
            strength[..., None] * value_blocks,
        ],
        axis=-1,
    )
    solved = forward_solve(lower_part, right_side)
    wide_keys = solved[..., :DK]
    base_values = solved[..., DK:]
    faded = jnp.exp(at_end - cumulative)[..., None] * key_blocks
    block_mult = jnp.exp(at_end)[..., None] * jnp.eye(DK, dtype=jnp.float32) - batch_stacked(
        "hbmk,hbmj->hbkj", faded, wide_keys
    )
    block_add = batch_stacked("hbmk,hbmv->hbkv", faded, base_values)
    read_slots = jnp.arange(block_tok) * NH + NH - 1
    visible = token_positions[None, :] <= read_slots[:, None]
    read_lag = jnp.where(visible, at_read[..., :, None] - cumulative[..., None, :], 0.0)
    read_weights = jnp.where(
        visible, jnp.exp(read_lag) * batch_stacked("hbtk,hbmk->hbtm", query_blocks, key_blocks), 0.0
    )
    query_eff = jnp.exp(at_read)[..., None] * query_blocks - batch_stacked(
        "hbtm,hbmk->hbtk", read_weights, wide_keys
    )
    local_out = batch_stacked("hbtm,hbmv->hbtv", read_weights, base_values)
    block_items = (
        jnp.moveaxis(block_mult, 1, 0),
        jnp.moveaxis(block_add, 1, 0),
        jnp.moveaxis(query_eff, 1, 0),
        jnp.moveaxis(local_out, 1, 0),
    )
    identity = jnp.broadcast_to(jnp.eye(DK, dtype=jnp.float32), (heads_here, DK, DK))
    zero_state = jnp.zeros((heads_here, DK, DV), jnp.float32)

    def join_block(running, pieces):
        prefix_mult, prefix_add = running
        step_mult, step_add = pieces
        updated = (
            batch_stacked("hij,hjk->hik", step_mult, prefix_mult),
            batch_stacked("hij,hjk->hik", step_mult, prefix_add) + step_add,
        )
        return (updated, None)

    (device_mult, device_add), _ = lax.scan(
        join_block, (identity, zero_state), (block_items[0], block_items[1])
    )

    def relay_step(round_index, incoming):
        outgoing = batch_stacked("hij,hjk->hik", device_mult, incoming) + device_add
        return shifted(outgoing, "seq", 1)

    state_in = lax.fori_loop(0, lax.axis_size("seq") - 1, relay_step, zero_state)

    def read_block(memory_state, pieces):
        step_mult, step_add, query_piece, local_piece = pieces
        output_block = local_piece + batch_stacked("xqu,xuj->xqj", query_piece, memory_state)
        return (batch_stacked("hij,hjk->hik", step_mult, memory_state) + step_add, output_block)

    _, out_rows = lax.scan(read_block, state_in, block_items)
    head_out = out_rows.transpose(0, 2, 1, 3).reshape(tok_local, heads_here, DV)
    inverse_rms = 1.0 / jnp.sqrt(jnp.mean(head_out * head_out, axis=-1, keepdims=True) + epsilon)
    gate_vals = jax.nn.silu(out_gate.astype(jnp.float32).reshape(tok_local, heads_here, DV))
    gated = (head_out * inverse_rms * norm_gain * gate_vals).astype(jnp.bfloat16)
    gated = gated.reshape(tok_local, heads_here * DV)
    mixed = jnp.dot(
        lax.all_gather(gated, "head", axis=1, tiled=True),
        out_weight,
        preferred_element_type=jnp.float32,
    )
    return mixed.astype(jnp.bfloat16)


def solution(mesh):
    return jax.shard_map(
        shards,
        mesh=mesh,
        in_specs=(
            P("seq", "head"),
            P("seq", None, "head"),
            P("seq", None, "head"),
            P(None, "head", "seq"),
            P("head", "seq"),
            P("seq"),
            P("seq", "head"),
            P(),
            P(None, "head"),
        ),
        out_specs=P("seq", "head"),
        check_vma=False,
    )
```

profile of v0, /device:TPU:0, one launch (start us, length us, event | category | flops | bytes accessed | tf_op | source)
XLA Modules:
  0.0 554.2 jit_solution(7442257994262153433)
XLA Ops:
  87.6 6.3 %bitcast_subtract_fusion = f32[2,16,128,128]{3,2,0,1:T(8,128)S(1)} fusion(f32[16,2,128,256]{3,2,1,0:T(8,128)} %copy-done.5, f32[16,2,128,128]{3,2,1,0:T(8,128)S(1)} %bitcast.213, f32[16,2,128]{2,1,0:T(2,128)S(1)} %copy.83, f32[128,128]{1,0:T(8,128)S(1)} %fusion.135, f32[2,16]{0,1:T(8,128)S(1)} %copy.82), kind=kOutput, calls=%fused_computation.47 | convolution fusion | flops 806879232 | bytes 6373504 | tf_op jit(solution)/shard_map/hbmk,hbmj->hbkj/dot_general | solution.py:26
  94.2 10.7 %while.37 = (s32[]{:T(128)}, f32[16,128,128]{2,1,0:T(8,128)S(1)}, f32[16,128,128]{2,1,0:T(8,128)}, f32[2,16,128,128]{3,2,1,0:T(8,128)S(1)}, f32[2,16,128,128]{3,2,1,0:T(8,128)}, /*index=5*/s32[]{:T(128)}, s32[]{:T(128)}) while((s32[]{:T(128)}, f32[16,128,128]{2,1,0:T(8,128)S(1)}, f32[16,128,128]{2,1,0:T(8,128)}, ...), condition=%wide.region_3.4_spmd.clone, body=%wide.region_2.0_spmd.clone.sunk | while | flops 805830656 | bytes 19924088 | solution.py:126
  106.0 393.8 %while.35 = (s32[]{:T(128)}, f32[16,128,128]{2,1,0:T(8,128)}, f32[16,128,128]{2,1,0:T(8,128)S(1)}, f32[16,128,128]{2,1,0:T(8,128)}, s32[]{:T(128)}) while((s32[]{:T(128)}, f32[16,128,128]{2,1,0:T(8,128)}, f32[16,128,128]{2,1,0:T(8,128)S(1)}, f32[16,128,128]{2,1,0:T(8,128)}, s32[]{:T(128)}) %tuple.84), condition=%wide.region_5.6_spmd, body=%wide.region_4.5_spmd.sunk | while | flops 402915328 | bytes 8388709 | solution.py:134
  115.5 21.7 %collective-permute-done = f32[16,128,128]{2,1,0:T(8,128)} collective-permute-done((f32[16,128,128]{2,1,0:T(8,128)}, f32[16,128,128]{2,1,0:T(8,128)}, u32[]{:S(2)}, u32[]{:S(2)}) %collective-permute-start) | collective-permute-done | bytes 1048608 | tf_op jit(solution)/shard_map/while/body/eval_jaxpr/ppermute | solution.py:18
  146.2 20.9 %collective-permute-done = f32[16,128,128]{2,1,0:T(8,128)} collective-permute-done((f32[16,128,128]{2,1,0:T(8,128)}, f32[16,128,128]{2,1,0:T(8,128)}, u32[]{:S(2)}, u32[]{:S(2)}) %collective-permute-start) | collective-permute-done | bytes 1048608 | tf_op jit(solution)/shard_map/while/body/eval_jaxpr/ppermute | solution.py:18
  176.1 19.9 %collective-permute-done = f32[16,128,128]{2,1,0:T(8,128)} collective-permute-done((f32[16,128,128]{2,1,0:T(8,128)}, f32[16,128,128]{2,1,0:T(8,128)}, u32[]{:S(2)}, u32[]{:S(2)}) %collective-permute-start) | collective-permute-done | bytes 1048608 | tf_op jit(solution)/shard_map/while/body/eval_jaxpr/ppermute | solution.py:18
  205.9 19.0 %collective-permute-done = f32[16,128,128]{2,1,0:T(8,128)} collective-permute-done((f32[16,128,128]{2,1,0:T(8,128)}, f32[16,128,128]{2,1,0:T(8,128)}, u32[]{:S(2)}, u32[]{:S(2)}) %collective-permute-start) | collective-permute-done | bytes 1048608 | tf_op jit(solution)/shard_map/while/body/eval_jaxpr/ppermute | solution.py:18
  228.6 6.3 %collective-permute-start = (f32[16,128,128]{2,1,0:T(8,128)}, f32[16,128,128]{2,1,0:T(8,128)}, u32[]{:S(2)}, u32[]{:S(2)}) collective-permute-start(f32[16,128,128]{2,1,0:T(8,128)} %convolution_add_fusion.31), channel_id=1, source_target_pairs={{0,2},{2,4},{4,6},{6,8},{8,10},{10,12},{12,14},{14,16},{16,18},{18... | collective-permute-start | bytes 3145736 | tf_op jit(solution)/shard_map/while/body/eval_jaxpr/ppermute | solution.py:18
  234.9 18.1 %collective-permute-done = f32[16,128,128]{2,1,0:T(8,128)} collective-permute-done((f32[16,128,128]{2,1,0:T(8,128)}, f32[16,128,128]{2,1,0:T(8,128)}, u32[]{:S(2)}, u32[]{:S(2)}) %collective-permute-start) | collective-permute-done | bytes 1048608 | tf_op jit(solution)/shard_map/while/body/eval_jaxpr/ppermute | solution.py:18
  256.6 6.3 %collective-permute-start = (f32[16,128,128]{2,1,0:T(8,128)}, f32[16,128,128]{2,1,0:T(8,128)}, u32[]{:S(2)}, u32[]{:S(2)}) collective-permute-start(f32[16,128,128]{2,1,0:T(8,128)} %convolution_add_fusion.31), channel_id=1, source_target_pairs={{0,2},{2,4},{4,6},{6,8},{8,10},{10,12},{12,14},{14,16},{16,18},{18... | collective-permute-start | bytes 3145736 | tf_op jit(solution)/shard_map/while/body/eval_jaxpr/ppermute | solution.py:18
  262.9 17.2 %collective-permute-done = f32[16,128,128]{2,1,0:T(8,128)} collective-permute-done((f32[16,128,128]{2,1,0:T(8,128)}, f32[16,128,128]{2,1,0:T(8,128)}, u32[]{:S(2)}, u32[]{:S(2)}) %collective-permute-start) | collective-permute-done | bytes 1048608 | tf_op jit(solution)/shard_map/while/body/eval_jaxpr/ppermute | solution.py:18
  283.8 6.3 %collective-permute-start = (f32[16,128,128]{2,1,0:T(8,128)}, f32[16,128,128]{2,1,0:T(8,128)}, u32[]{:S(2)}, u32[]{:S(2)}) collective-permute-start(f32[16,128,128]{2,1,0:T(8,128)} %convolution_add_fusion.31), channel_id=1, source_target_pairs={{0,2},{2,4},{4,6},{6,8},{8,10},{10,12},{12,14},{14,16},{16,18},{18... | collective-permute-start | bytes 3145736 | tf_op jit(solution)/shard_map/while/body/eval_jaxpr/ppermute | solution.py:18
  290.0 16.3 %collective-permute-done = f32[16,128,128]{2,1,0:T(8,128)} collective-permute-done((f32[16,128,128]{2,1,0:T(8,128)}, f32[16,128,128]{2,1,0:T(8,128)}, u32[]{:S(2)}, u32[]{:S(2)}) %collective-permute-start) | collective-permute-done | bytes 1048608 | tf_op jit(solution)/shard_map/while/body/eval_jaxpr/ppermute | solution.py:18
  309.9 6.3 %collective-permute-start = (f32[16,128,128]{2,1,0:T(8,128)}, f32[16,128,128]{2,1,0:T(8,128)}, u32[]{:S(2)}, u32[]{:S(2)}) collective-permute-start(f32[16,128,128]{2,1,0:T(8,128)} %convolution_add_fusion.31), channel_id=1, source_target_pairs={{0,2},{2,4},{4,6},{6,8},{8,10},{10,12},{12,14},{14,16},{16,18},{18... | collective-permute-start | bytes 3145736 | tf_op jit(solution)/shard_map/while/body/eval_jaxpr/ppermute | solution.py:18
  316.2 15.3 %collective-permute-done = f32[16,128,128]{2,1,0:T(8,128)} collective-permute-done((f32[16,128,128]{2,1,0:T(8,128)}, f32[16,128,128]{2,1,0:T(8,128)}, u32[]{:S(2)}, u32[]{:S(2)}) %collective-permute-start) | collective-permute-done | bytes 1048608 | tf_op jit(solution)/shard_map/while/body/eval_jaxpr/ppermute | solution.py:18
  335.2 7.0 %collective-permute-start = (f32[16,128,128]{2,1,0:T(8,128)}, f32[16,128,128]{2,1,0:T(8,128)}, u32[]{:S(2)}, u32[]{:S(2)}) collective-permute-start(f32[16,128,128]{2,1,0:T(8,128)} %convolution_add_fusion.31), channel_id=1, source_target_pairs={{0,2},{2,4},{4,6},{6,8},{8,10},{10,12},{12,14},{14,16},{16,18},{18... | collective-permute-start | bytes 3145736 | tf_op jit(solution)/shard_map/while/body/eval_jaxpr/ppermute | solution.py:18
  342.2 14.4 %collective-permute-done = f32[16,128,128]{2,1,0:T(8,128)} collective-permute-done((f32[16,128,128]{2,1,0:T(8,128)}, f32[16,128,128]{2,1,0:T(8,128)}, u32[]{:S(2)}, u32[]{:S(2)}) %collective-permute-start) | collective-permute-done | bytes 1048608 | tf_op jit(solution)/shard_map/while/body/eval_jaxpr/ppermute | solution.py:18
  360.3 7.2 %collective-permute-start = (f32[16,128,128]{2,1,0:T(8,128)}, f32[16,128,128]{2,1,0:T(8,128)}, u32[]{:S(2)}, u32[]{:S(2)}) collective-permute-start(f32[16,128,128]{2,1,0:T(8,128)} %convolution_add_fusion.31), channel_id=1, source_target_pairs={{0,2},{2,4},{4,6},{6,8},{8,10},{10,12},{12,14},{14,16},{16,18},{18... | collective-permute-start | bytes 3145736 | tf_op jit(solution)/shard_map/while/body/eval_jaxpr/ppermute | solution.py:18
  367.4 13.5 %collective-permute-done = f32[16,128,128]{2,1,0:T(8,128)} collective-permute-done((f32[16,128,128]{2,1,0:T(8,128)}, f32[16,128,128]{2,1,0:T(8,128)}, u32[]{:S(2)}, u32[]{:S(2)}) %collective-permute-start) | collective-permute-done | bytes 1048608 | tf_op jit(solution)/shard_map/while/body/eval_jaxpr/ppermute | solution.py:18
  384.6 7.2 %collective-permute-start = (f32[16,128,128]{2,1,0:T(8,128)}, f32[16,128,128]{2,1,0:T(8,128)}, u32[]{:S(2)}, u32[]{:S(2)}) collective-permute-start(f32[16,128,128]{2,1,0:T(8,128)} %convolution_add_fusion.31), channel_id=1, source_target_pairs={{0,2},{2,4},{4,6},{6,8},{8,10},{10,12},{12,14},{14,16},{16,18},{18... | collective-permute-start | bytes 3145736 | tf_op jit(solution)/shard_map/while/body/eval_jaxpr/ppermute | solution.py:18
  391.8 12.6 %collective-permute-done = f32[16,128,128]{2,1,0:T(8,128)} collective-permute-done((f32[16,128,128]{2,1,0:T(8,128)}, f32[16,128,128]{2,1,0:T(8,128)}, u32[]{:S(2)}, u32[]{:S(2)}) %collective-permute-start) | collective-permute-done | bytes 1048608 | tf_op jit(solution)/shard_map/while/body/eval_jaxpr/ppermute | solution.py:18
  408.0 7.2 %collective-permute-start = (f32[16,128,128]{2,1,0:T(8,128)}, f32[16,128,128]{2,1,0:T(8,128)}, u32[]{:S(2)}, u32[]{:S(2)}) collective-permute-start(f32[16,128,128]{2,1,0:T(8,128)} %convolution_add_fusion.31), channel_id=1, source_target_pairs={{0,2},{2,4},{4,6},{6,8},{8,10},{10,12},{12,14},{14,16},{16,18},{18... | collective-permute-start | bytes 3145736 | tf_op jit(solution)/shard_map/while/body/eval_jaxpr/ppermute | solution.py:18
  415.2 12.4 %collective-permute-done = f32[16,128,128]{2,1,0:T(8,128)} collective-permute-done((f32[16,128,128]{2,1,0:T(8,128)}, f32[16,128,128]{2,1,0:T(8,128)}, u32[]{:S(2)}, u32[]{:S(2)}) %collective-permute-start) | collective-permute-done | bytes 1048608 | tf_op jit(solution)/shard_map/while/body/eval_jaxpr/ppermute | solution.py:18
  431.3 7.2 %collective-permute-start = (f32[16,128,128]{2,1,0:T(8,128)}, f32[16,128,128]{2,1,0:T(8,128)}, u32[]{:S(2)}, u32[]{:S(2)}) collective-permute-start(f32[16,128,128]{2,1,0:T(8,128)} %convolution_add_fusion.31), channel_id=1, source_target_pairs={{0,2},{2,4},{4,6},{6,8},{8,10},{10,12},{12,14},{14,16},{16,18},{18... | collective-permute-start | bytes 3145736 | tf_op jit(solution)/shard_map/while/body/eval_jaxpr/ppermute | solution.py:18
  438.4 13.2 %collective-permute-done = f32[16,128,128]{2,1,0:T(8,128)} collective-permute-done((f32[16,128,128]{2,1,0:T(8,128)}, f32[16,128,128]{2,1,0:T(8,128)}, u32[]{:S(2)}, u32[]{:S(2)}) %collective-permute-start) | collective-permute-done | bytes 1048608 | tf_op jit(solution)/shard_map/while/body/eval_jaxpr/ppermute | solution.py:18
  455.3 7.2 %collective-permute-start = (f32[16,128,128]{2,1,0:T(8,128)}, f32[16,128,128]{2,1,0:T(8,128)}, u32[]{:S(2)}, u32[]{:S(2)}) collective-permute-start(f32[16,128,128]{2,1,0:T(8,128)} %convolution_add_fusion.31), channel_id=1, source_target_pairs={{0,2},{2,4},{4,6},{6,8},{8,10},{10,12},{12,14},{14,16},{16,18},{18... | collective-permute-start | bytes 3145736 | tf_op jit(solution)/shard_map/while/body/eval_jaxpr/ppermute | solution.py:18
  462.5 14.0 %collective-permute-done = f32[16,128,128]{2,1,0:T(8,128)} collective-permute-done((f32[16,128,128]{2,1,0:T(8,128)}, f32[16,128,128]{2,1,0:T(8,128)}, u32[]{:S(2)}, u32[]{:S(2)}) %collective-permute-start) | collective-permute-done | bytes 1048608 | tf_op jit(solution)/shard_map/while/body/eval_jaxpr/ppermute | solution.py:18
  480.1 8.0 %collective-permute-start = (f32[16,128,128]{2,1,0:T(8,128)}, f32[16,128,128]{2,1,0:T(8,128)}, u32[]{:S(2)}, u32[]{:S(2)}) collective-permute-start(f32[16,128,128]{2,1,0:T(8,128)} %convolution_add_fusion.31), channel_id=1, source_target_pairs={{0,2},{2,4},{4,6},{6,8},{8,10},{10,12},{12,14},{14,16},{16,18},{18... | collective-permute-start | bytes 3145736 | tf_op jit(solution)/shard_map/while/body/eval_jaxpr/ppermute | solution.py:18
  488.2 11.6 %collective-permute-done = f32[16,128,128]{2,1,0:T(8,128)} collective-permute-done((f32[16,128,128]{2,1,0:T(8,128)}, f32[16,128,128]{2,1,0:T(8,128)}, u32[]{:S(2)}, u32[]{:S(2)}) %collective-permute-start) | collective-permute-done | bytes 1048608 | tf_op jit(solution)/shard_map/while/body/eval_jaxpr/ppermute | solution.py:18
  499.8 12.0 %while.36 = (s32[]{:T(128)}, f32[16,128,128]{2,1,0:T(8,128)}, f32[2,16,64,128]{3,2,1,0:T(8,128)}, f32[2,16,128,128]{3,2,1,0:T(8,128)S(1)}, f32[2,16,128,128]{3,2...) while((s32[]{:T(128)}, f32[16,128,128]{2,1,0:T(8,128)}, ...), condition=%wide.region_8.9_spmd, body=%wide.region_7.8_spmd.sunk | while | flops 604372992 | bytes 25692328 | solution.py:141
  517.5 20.5 %all-gather.2.cloned.1.call-done = bf16[128,4096]{1,0:T(8,128)(2,1)} async-done(((bf16[128,2048]{1,0:T(8,128)(2,1)}), bf16[128,4096]{1,0:T(8,128)(2,1)}) %all-gather.2.cloned.1.call-update) | async-done | bytes 1048592 | tf_op jit(solution)/shard_map/all_gather | solution.py:148
  537.9 9.2 %convolution_convert_fusion = bf16[128,2048]{1,0:T(8,128)(2,1)} fusion(bf16[128,4096]{1,0:T(8,128)(2,1)} %all-gather.2.cloned.1.call-done, bf16[4096,2048]{1,0:T(8,128)(2,1)} %param.23), kind=kOutput, calls=%fused_computation.37 | convolution fusion | flops 2147745792 | bytes 18350080 | tf_op jit(solution)/shard_map/dot_general | solution.py:147
  (203 shorter events, 187.4 us)
Async XLA Ops:
  6.5 508.8 %copy-start = (f32[128]{0:T(128)S(1)}, f32[128]{0:T(128)}, u32[]{:S(2)}) copy-start(f32[128]{0:T(128)} %param.22) | copy-start | bytes 1540
  6.5 531.4 %all-gather.2.cloned.1.call-start = ((), (), s32[]{:S(2)}) async-start(), calls=%async_computation | async-start | bytes 1572864 | tf_op jit(solution)/shard_map/all_gather | solution.py:148
  19.6 17.4 %copy-start.3 = (f32[16,2,128,128]{3,2,1,0:T(8,128)}, f32[16,2,128,128]{3,2,1,0:T(8,128)S(1)}, u32[]{:S(2)}) copy-start(f32[16,2,128,128]{3,2,1,0:T(8,128)S(1)} %multiply_select_fusion) | copy-start | bytes 6291460
  39.5 3.8 copy-start.10
  46.1 1.6 copy-start.4
  59.1 2.0 copy-start.13
  62.5 2.0 copy-start.12
  65.9 2.3 copy-start.11
  65.9 2.7 copy-start.18
  71.0 10.7 %copy-start.5 = (f32[16,2,128,256]{3,2,1,0:T(8,128)}, f32[16,2,128,256]{3,2,1,0:T(8,128)S(1)}, u32[]{:S(2)}) copy-start(f32[16,2,128,256]{3,2,1,0:T(8,128)S(1)} %convolution_dynamic-update-slice_fusion) | copy-start | bytes 12582916
  94.2 1.9 copy-start.1
  99.5 1.9 copy-start.1
  109.7 27.6 %collective-permute-start = (f32[16,128,128]{2,1,0:T(8,128)}, f32[16,128,128]{2,1,0:T(8,128)}, u32[]{:S(2)}, u32[]{:S(2)}) collective-permute-start(f32[16,128,128]{2,1,0:T(8,128)} %convolution_add_fusion.31), channel_id=1, source_target_pairs={{0,2},{2,4},{4,6},{6,8},{8,10},{10,12},{12,14},{14,16},{16,18},{18... | collective-permute-start | bytes 3145736 | tf_op jit(solution)/shard_map/while/body/eval_jaxpr/ppermute | solution.py:18
  140.9 26.2 %collective-permute-start = (f32[16,128,128]{2,1,0:T(8,128)}, f32[16,128,128]{2,1,0:T(8,128)}, u32[]{:S(2)}, u32[]{:S(2)}) collective-permute-start(f32[16,128,128]{2,1,0:T(8,128)} %convolution_add_fusion.31), channel_id=1, source_target_pairs={{0,2},{2,4},{4,6},{6,8},{8,10},{10,12},{12,14},{14,16},{16,18},{18... | collective-permute-start | bytes 3145736 | tf_op jit(solution)/shard_map/while/body/eval_jaxpr/ppermute | solution.py:18
  170.8 25.3 %collective-permute-start = (f32[16,128,128]{2,1,0:T(8,128)}, f32[16,128,128]{2,1,0:T(8,128)}, u32[]{:S(2)}, u32[]{:S(2)}) collective-permute-start(f32[16,128,128]{2,1,0:T(8,128)} %convolution_add_fusion.31), channel_id=1, source_target_pairs={{0,2},{2,4},{4,6},{6,8},{8,10},{10,12},{12,14},{14,16},{16,18},{18... | collective-permute-start | bytes 3145736 | tf_op jit(solution)/shard_map/while/body/eval_jaxpr/ppermute | solution.py:18
  199.8 25.2 %collective-permute-start = (f32[16,128,128]{2,1,0:T(8,128)}, f32[16,128,128]{2,1,0:T(8,128)}, u32[]{:S(2)}, u32[]{:S(2)}) collective-permute-start(f32[16,128,128]{2,1,0:T(8,128)} %convolution_add_fusion.31), channel_id=1, source_target_pairs={{0,2},{2,4},{4,6},{6,8},{8,10},{10,12},{12,14},{14,16},{16,18},{18... | collective-permute-start | bytes 3145736 | tf_op jit(solution)/shard_map/while/body/eval_jaxpr/ppermute | solution.py:18
  228.6 24.4 %collective-permute-start = (f32[16,128,128]{2,1,0:T(8,128)}, f32[16,128,128]{2,1,0:T(8,128)}, u32[]{:S(2)}, u32[]{:S(2)}) collective-permute-start(f32[16,128,128]{2,1,0:T(8,128)} %convolution_add_fusion.31), channel_id=1, source_target_pairs={{0,2},{2,4},{4,6},{6,8},{8,10},{10,12},{12,14},{14,16},{16,18},{18... | collective-permute-start | bytes 3145736 | tf_op jit(solution)/shard_map/while/body/eval_jaxpr/ppermute | solution.py:18
  256.6 23.4 %collective-permute-start = (f32[16,128,128]{2,1,0:T(8,128)}, f32[16,128,128]{2,1,0:T(8,128)}, u32[]{:S(2)}, u32[]{:S(2)}) collective-permute-start(f32[16,128,128]{2,1,0:T(8,128)} %convolution_add_fusion.31), channel_id=1, source_target_pairs={{0,2},{2,4},{4,6},{6,8},{8,10},{10,12},{12,14},{14,16},{16,18},{18... | collective-permute-start | bytes 3145736 | tf_op jit(solution)/shard_map/while/body/eval_jaxpr/ppermute | solution.py:18
  283.8 22.5 %collective-permute-start = (f32[16,128,128]{2,1,0:T(8,128)}, f32[16,128,128]{2,1,0:T(8,128)}, u32[]{:S(2)}, u32[]{:S(2)}) collective-permute-start(f32[16,128,128]{2,1,0:T(8,128)} %convolution_add_fusion.31), channel_id=1, source_target_pairs={{0,2},{2,4},{4,6},{6,8},{8,10},{10,12},{12,14},{14,16},{16,18},{18... | collective-permute-start | bytes 3145736 | tf_op jit(solution)/shard_map/while/body/eval_jaxpr/ppermute | solution.py:18
  309.9 21.6 %collective-permute-start = (f32[16,128,128]{2,1,0:T(8,128)}, f32[16,128,128]{2,1,0:T(8,128)}, u32[]{:S(2)}, u32[]{:S(2)}) collective-permute-start(f32[16,128,128]{2,1,0:T(8,128)} %convolution_add_fusion.31), channel_id=1, source_target_pairs={{0,2},{2,4},{4,6},{6,8},{8,10},{10,12},{12,14},{14,16},{16,18},{18... | collective-permute-start | bytes 3145736 | tf_op jit(solution)/shard_map/while/body/eval_jaxpr/ppermute | solution.py:18
  335.2 21.4 %collective-permute-start = (f32[16,128,128]{2,1,0:T(8,128)}, f32[16,128,128]{2,1,0:T(8,128)}, u32[]{:S(2)}, u32[]{:S(2)}) collective-permute-start(f32[16,128,128]{2,1,0:T(8,128)} %convolution_add_fusion.31), channel_id=1, source_target_pairs={{0,2},{2,4},{4,6},{6,8},{8,10},{10,12},{12,14},{14,16},{16,18},{18... | collective-permute-start | bytes 3145736 | tf_op jit(solution)/shard_map/while/body/eval_jaxpr/ppermute | solution.py:18
  360.3 20.7 %collective-permute-start = (f32[16,128,128]{2,1,0:T(8,128)}, f32[16,128,128]{2,1,0:T(8,128)}, u32[]{:S(2)}, u32[]{:S(2)}) collective-permute-start(f32[16,128,128]{2,1,0:T(8,128)} %convolution_add_fusion.31), channel_id=1, source_target_pairs={{0,2},{2,4},{4,6},{6,8},{8,10},{10,12},{12,14},{14,16},{16,18},{18... | collective-permute-start | bytes 3145736 | tf_op jit(solution)/shard_map/while/body/eval_jaxpr/ppermute | solution.py:18
  384.6 19.7 %collective-permute-start = (f32[16,128,128]{2,1,0:T(8,128)}, f32[16,128,128]{2,1,0:T(8,128)}, u32[]{:S(2)}, u32[]{:S(2)}) collective-permute-start(f32[16,128,128]{2,1,0:T(8,128)} %convolution_add_fusion.31), channel_id=1, source_target_pairs={{0,2},{2,4},{4,6},{6,8},{8,10},{10,12},{12,14},{14,16},{16,18},{18... | collective-permute-start | bytes 3145736 | tf_op jit(solution)/shard_map/while/body/eval_jaxpr/ppermute | solution.py:18
  408.0 19.6 %collective-permute-start = (f32[16,128,128]{2,1,0:T(8,128)}, f32[16,128,128]{2,1,0:T(8,128)}, u32[]{:S(2)}, u32[]{:S(2)}) collective-permute-start(f32[16,128,128]{2,1,0:T(8,128)} %convolution_add_fusion.31), channel_id=1, source_target_pairs={{0,2},{2,4},{4,6},{6,8},{8,10},{10,12},{12,14},{14,16},{16,18},{18... | collective-permute-start | bytes 3145736 | tf_op jit(solution)/shard_map/while/body/eval_jaxpr/ppermute | solution.py:18
  431.3 20.4 %collective-permute-start = (f32[16,128,128]{2,1,0:T(8,128)}, f32[16,128,128]{2,1,0:T(8,128)}, u32[]{:S(2)}, u32[]{:S(2)}) collective-permute-start(f32[16,128,128]{2,1,0:T(8,128)} %convolution_add_fusion.31), channel_id=1, source_target_pairs={{0,2},{2,4},{4,6},{6,8},{8,10},{10,12},{12,14},{14,16},{16,18},{18... | collective-permute-start | bytes 3145736 | tf_op jit(solution)/shard_map/while/body/eval_jaxpr/ppermute | solution.py:18
  455.3 21.2 %collective-permute-start = (f32[16,128,128]{2,1,0:T(8,128)}, f32[16,128,128]{2,1,0:T(8,128)}, u32[]{:S(2)}, u32[]{:S(2)}) collective-permute-start(f32[16,128,128]{2,1,0:T(8,128)} %convolution_add_fusion.31), channel_id=1, source_target_pairs={{0,2},{2,4},{4,6},{6,8},{8,10},{10,12},{12,14},{14,16},{16,18},{18... | collective-permute-start | bytes 3145736 | tf_op jit(solution)/shard_map/while/body/eval_jaxpr/ppermute | solution.py:18
  480.1 19.7 %collective-permute-start = (f32[16,128,128]{2,1,0:T(8,128)}, f32[16,128,128]{2,1,0:T(8,128)}, u32[]{:S(2)}, u32[]{:S(2)}) collective-permute-start(f32[16,128,128]{2,1,0:T(8,128)} %convolution_add_fusion.31), channel_id=1, source_target_pairs={{0,2},{2,4},{4,6},{6,8},{8,10},{10,12},{12,14},{14,16},{16,18},{18... | collective-permute-start | bytes 3145736 | tf_op jit(solution)/shard_map/while/body/eval_jaxpr/ppermute | solution.py:18
  499.8 1.9 copy-start.7
  499.8 3.8 copy-start.2
  505.7 1.9 copy-start.7
  505.7 3.7 copy-start.2
  511.8 3.9 copy-start.19
  (9 other events, 11.3 us)
Sparse Core Ops, SparseCore 0:
  517.6 20.2 all-gather.1
where the time goes:
time: 565 us; the launch traced here: 554 us
  waiting for transfers between devices  261 us (46%)
  matrix products  149 us (26%)
  starting transfers between devices  98.6 us (17%)
  local copies, waits for them, and re-layouts  20.6 us (4%)
  between operations  14.4 us (3%)
  other arithmetic  11.1 us (2%)
    ppermute x15, waiting for transfers between devices, shifted(): return lax.ppermute(shard, axis, pairs)  240 us
    ppermute x15, starting transfers between devices, shifted(): return lax.ppermute(shard, axis, pairs)  98.6 us
    dot_general x29, matrix products, batch_stacked(): jnp.einsum(einsum_form, left_side, right_hand, precision=highest_precision)  95.7 us
    dot_general x63, matrix products, stacked_product(): return jnp.matmul(left_side, right_hand, precision=highest_precision)  43.7 us
    all_gather x1, waiting for transfers between devices, shards(): lax.all_gather(gated, 'head', axis=1, tiled=True)  20.5 us
  transfers between devices with their start and end apart: 16, of which 16 were waited for; matrix products, arithmetic and copies ran while one was open for 0% of the time, Pallas kernels for 0%

commit v1 on v0

v1 whole, which is shorter than its diff:
```python
import functools

import jax
import jax.numpy as jnp
from jax import lax
from jax.experimental import pallas as pl
from jax.experimental.pallas import tpu as pltpu
from jax.sharding import PartitionSpec as P

DK = 128
NH = 2
EPS = 1e-06
F32 = jnp.float32
BF16 = jnp.bfloat16
MESH = pl.DeviceIdType.MESH
MIB = 1024 * 1024


def mm(a, b):
    return jnp.dot(a, b, preferred_element_type=F32)


def mm_t(a, b):
    return lax.dot_general(a, b, (((1,), (1,)), ((), ())), preferred_element_type=F32)


def t_mm(a, b):
    return lax.dot_general(a, b, (((0,), (0,)), ((), ())), preferred_element_type=F32)


def split(x):
    hi = x.astype(BF16)
    return hi, (x - hi.astype(F32)).astype(BF16)


def step_times(shape, axis, tok):
    index = lax.broadcasted_iota(jnp.int32, shape, axis)
    return jnp.where(index < tok, NH * index, NH * (index - tok) + 1)


def prepare(kb, vb, qb, cum_col, cum_row, s_col, s_row):
    tok = qb.shape[0]
    steps = NH * tok
    row_time = step_times((steps, steps), 0, tok)
    col_time = step_times((steps, steps), 1, tok)
    apart = row_time ^ col_time
    strictly = row_time > col_time
    diagonal = row_time == col_time

    gram = mm_t(kb, kb)
    on_diag = jnp.where(diagonal, gram, 0.0)
    rk_row = lax.rsqrt(jnp.sum(on_diag, axis=0, keepdims=True) + EPS)
    rk_col = lax.rsqrt(jnp.sum(on_diag, axis=1, keepdims=True) + EPS)
    qf = qb.astype(F32)
    rq_col = lax.rsqrt(jnp.sum(qf * qf, axis=1, keepdims=True) + EPS)

    small_row = lax.broadcasted_iota(jnp.int32, (tok, tok), 0)
    small_col = lax.broadcasted_iota(jnp.int32, (tok, tok), 1)
    seen = small_row >= small_col
    decay = jnp.where(seen, jnp.exp(jnp.where(seen, cum_col - cum_row, 0.0)), 0.0)
    decay_wide = jnp.concatenate([decay, decay], axis=1)
    decay_full = jnp.concatenate([decay_wide, decay_wide], axis=0)
    cum2_row = jnp.concatenate([cum_row, cum_row], axis=1)
    cum2_col = jnp.concatenate([cum_col, cum_col], axis=0)
    end = cum_row[:, tok - 1 : tok]

    lower = jnp.where(strictly, (s_col * rk_col) * (gram * decay_full) * rk_row, 0.0)
    lower_hi, lower_lo = split(lower)
    unit = jnp.where(diagonal, 1.0, 0.0)
    inverse = unit - jnp.where(apart == 1, lower, 0.0)
    width = 2
    while width < steps:
        corner = jnp.where((apart >= width) & (apart < 2 * width), lower, 0.0).astype(BF16)
        rounded = inverse.astype(BF16)
        inverse = inverse - mm(mm(rounded, corner).astype(BF16), rounded)
        width *= 2
    inv_hi, inv_lo = split(inverse)
    residual = unit - inverse - (mm(lower_hi, inv_hi) + (mm(lower_hi, inv_lo) + mm(lower_lo, inv_hi)))
    inverse = inverse + mm(inv_hi, residual.astype(BF16))

    by_value = inverse * s_row
    val_hi, val_lo = split(by_value)
    key_hi, key_lo = split(by_value * (jnp.exp(cum2_row) * rk_row))
    solved = jnp.concatenate([mm(key_hi, kb) + mm(key_lo, kb), mm(val_hi, vb) + mm(val_lo, vb)], axis=1)
    solved_hi, solved_lo = split(solved)
    faded_hi, faded_lo = split((jnp.exp(end - cum2_col) * rk_col) * solved)
    carried = t_mm(kb, faded_hi) + t_mm(kb, faded_lo)
    mult = jnp.where(small_row == small_col, jnp.exp(end), 0.0) - carried[:, :DK]

    weights = (rq_col * rk_row) * (decay_wide * mm_t(qb, kb))
    w_hi, w_lo = split(weights)
    read = mm(w_hi, solved_hi) + (mm(w_hi, solved_lo) + mm(w_lo, solved_hi))
    query_eff = (jnp.exp(cum_col) * rq_col) * qf - read[:, :DK]
    maps = jnp.concatenate([mult, query_eff], axis=0)
    adds = jnp.concatenate([carried[:, DK:], read[:, DK:]], axis=0)
    return maps, adds


def prepare_kernel(together, k_ref, v_ref, q_ref, cumt_ref, st_ref, cum_ref, s_ref, hi_ref, lo_ref, add_ref):
    def column(ref, head):
        lane = lax.broadcasted_iota(jnp.int32, ref.shape, 1)
        return jnp.sum(jnp.where(lane == head, ref[...], 0.0), axis=1, keepdims=True)

    for i in range(together):
        head = pl.program_id(0) * together + i
        cols = slice(i * DK, (i + 1) * DK)
        maps, adds = prepare(
            k_ref[:, cols], v_ref[:, cols], q_ref[:, cols],
            column(cumt_ref, head), cum_ref[i], column(st_ref, head), s_ref[i],
        )
        hi_ref[i], lo_ref[i] = split(maps)
        add_ref[i] = adds


def relay_kernel(
    n, heads, group, hi_ref, lo_ref, add_ref, gate_ref, gain_ref, w_ref, out_ref,
    w_vmem, arrived, leaving, gated, total,
    w_sem, send_sem, recv_sem, gsend_sem, grecv_sem,
):
    me = lax.axis_index("seq")
    core = lax.axis_index("head")
    tok = gate_ref.shape[1]
    right, left = lax.rem(me + 1, n), lax.rem(me + n - 1, n)
    other = 1 - core

    load = pltpu.make_async_copy(w_ref, w_vmem, w_sem)
    load.start()
    barrier = pltpu.get_barrier_semaphore()
    pl.semaphore_signal(barrier, inc=1, device_id=(left, core), device_id_type=MESH)
    pl.semaphore_signal(barrier, inc=1, device_id=(me, other), device_id_type=MESH)

    @pl.when(me == 0)
    def _():
        arrived[...] = jnp.zeros_like(arrived)

    pl.semaphore_wait(barrier, 2)

    def onward(h):
        return pltpu.make_async_remote_copy(
            src_ref=leaving.at[h], dst_ref=arrived.at[h], send_sem=send_sem.at[h], recv_sem=recv_sem.at[h],
            device_id=(right, core), device_id_type=MESH,
        )

    def across(h):
        slot = gated.at[core * heads + h]
        return pltpu.make_async_remote_copy(
            src_ref=slot, dst_ref=slot, send_sem=gsend_sem.at[h], recv_sem=grecv_sem.at[h],
            device_id=(me, other), device_id_type=MESH,
        )

    @pl.loop(0, heads)
    def _(h):
        @pl.when(me > 0)
        def _():
            onward(h).wait_recv()

        s_hi, s_lo = split(arrived[h])
        both = mm(hi_ref[h], jnp.concatenate([s_hi, s_lo], axis=1))
        result = (both[:, :DK] + (both[:, DK:] + mm(lo_ref[h], s_hi))) + add_ref[h]
        leaving[h] = result[:DK]

        @pl.when(me < n - 1)
        def _():
            onward(h).start()

        rows = result[DK:]
        scale = lax.rsqrt(jnp.mean(rows * rows, axis=1, keepdims=True) + EPS)
        x = gate_ref[h].astype(F32)
        gated[core * heads + h] = (rows * scale * gain_ref[...] * (x / (1.0 + jnp.exp(-x)))).astype(BF16)
        across(h).start()

    load.wait()
    total[...] = jnp.zeros_like(total)

    @pl.loop(0, heads)
    def _(h):
        across(h).wait_recv()

    @pl.loop(0, 2 * heads // group)
    def _(g):
        block = jnp.concatenate([gated[g * group + i] for i in range(group)], axis=1)
        total[...] += mm(block, w_vmem[pl.ds(pl.multiple_of(g * group * DK, group * DK), group * DK), :])

    out_ref[...] = total[...].astype(out_ref.dtype)

    @pl.loop(0, heads)
    def _(h):
        across(h).wait_send()

        @pl.when(me < n - 1)
        def _():
            onward(h).wait_send()


def shards(n, query, keys, values, beta, gate_log, house_count, out_gate, norm_gain, out_weight):
    tok = query.shape[0]
    heads = query.shape[1] // DK
    steps = NH * tok
    width = out_weight.shape[1]
    active = (jnp.arange(NH, dtype=jnp.int32)[:, None] < house_count[None, :]).astype(F32)
    strength = (beta * active[:, None, :]).transpose(1, 0, 2).reshape(heads, steps)
    upper = (jnp.arange(tok)[:, None] <= jnp.arange(tok)[None, :]).astype(F32)
    cum = jnp.dot(gate_log, upper, precision=lax.Precision.HIGHEST)
    k2 = keys.transpose(1, 0, 2).reshape(steps, heads * DK)
    v2 = values.transpose(1, 0, 2).reshape(steps, heads * DK)
    gate3 = out_gate.reshape(tok, heads, DK).transpose(1, 0, 2)

    together = 2
    maps_hi, maps_lo, adds = pl.pallas_call(
        functools.partial(prepare_kernel, together),
        grid=(heads // together,),
        in_specs=[
            pl.BlockSpec((steps, together * DK), lambda i: (0, i)),
            pl.BlockSpec((steps, together * DK), lambda i: (0, i)),
            pl.BlockSpec((tok, together * DK), lambda i: (0, i)),
            pl.BlockSpec((tok, heads), lambda i: (0, 0)),
            pl.BlockSpec((steps, heads), lambda i: (0, 0)),
            pl.BlockSpec((together, 1, tok), lambda i: (i, 0, 0)),
            pl.BlockSpec((together, 1, steps), lambda i: (i, 0, 0)),
        ],
        out_specs=[pl.BlockSpec((together, DK + tok, DK), lambda i: (i, 0, 0))] * 3,
        out_shape=[jax.ShapeDtypeStruct((heads, DK + tok, DK), t) for t in (BF16, BF16, F32)],
        compiler_params=pltpu.CompilerParams(vmem_limit_bytes=40 * MIB),
    )(k2, v2, query, cum.T, strength.T, cum[:, None, :], strength[:, None, :])

    group = 4
    vmem = pl.BlockSpec(memory_space=pltpu.VMEM)
    return pl.pallas_call(
        functools.partial(relay_kernel, n, heads, group),
        in_specs=[vmem] * 5 + [pl.BlockSpec(memory_space=pl.ANY)],
        out_specs=vmem,
        out_shape=jax.ShapeDtypeStruct((tok, width), BF16),
        scratch_shapes=[
            pltpu.VMEM(out_weight.shape, BF16),
            pltpu.VMEM((heads, DK, DK), F32),
            pltpu.VMEM((heads, DK, DK), F32),
            pltpu.VMEM((2 * heads, tok, DK), BF16),
            pltpu.VMEM((tok, width), F32),
            pltpu.SemaphoreType.DMA,
            pltpu.SemaphoreType.DMA((heads,)),
            pltpu.SemaphoreType.DMA((heads,)),
            pltpu.SemaphoreType.DMA((heads,)),
            pltpu.SemaphoreType.DMA((heads,)),
        ],
        compiler_params=pltpu.CompilerParams(
            collective_id=0, has_side_effects=True, vmem_limit_bytes=56 * MIB
        ),
    )(maps_hi, maps_lo, adds, gate3, norm_gain[None, :], out_weight)


def solution(mesh):
    return jax.shard_map(
        functools.partial(shards, mesh.shape["seq"]),
        mesh=mesh,
        in_specs=(
            P("seq", "head"),
            P("seq", None, "head"),
            P("seq", None, "head"),
            P(None, "head", "seq"),
            P("head", "seq"),
            P("seq"),
            P("seq", "head"),
            P(),
            P(None, "head"),
        ),
        out_specs=P("seq", "head"),
        check_vma=False,
    )
```

time: 565 us -> 149 us (0.26)
  the two profiles are of different devices: /device:TPU:0 before, /device:TPU:30 now
where the time goes in v1:
time: 149 us; the launch traced here: 147 us
  Pallas kernels  133 us (89%)
  local copies, waits for them, and re-layouts  11.9 us (8%)
    pallas_call x1, Pallas kernels, shards(): pl.pallas_call(functools.partial(relay_kernel, n, heads, group), in_specs...  85.7 us
    pallas_call x1, Pallas kernels, shards(): pl.pallas_call(functools.partial(prepare_kernel, together), grid=(heads /...  47.8 us
    unnamed x12, local copies, waits for them, and re-layouts  7.53 us

profile of v1, /device:TPU:30, one launch (start us, length us, event | category | flops | bytes accessed | tf_op | source)
XLA Modules:
  0.0 147.0 jit_solution(15108142736831172708)
XLA Ops:
  0.0 0.0 copy-start
  0.0 0.7 compare_convert_fusion
  0.7 0.7 multiply_bitcast_fusion
  1.4 0.1 copy.17
  1.5 0.0 copy-done
  1.5 0.1 fusion
  1.6 0.1 copy.19.cumt_ref
  1.8 1.6 %copy.15 = bf16[2,128,2048]{2,1,0:T(8,128)(2,1)S(1)} copy(bf16[2,128,2048]{2,0,1:T(2,128)(2,1)} %bitcast.24) | data formatting | bytes 2097152 | tf_op jit(solution)/shard_map/transpose | solution.py:204
  3.4 1.6 %copy.16 = bf16[2,128,2048]{2,1,0:T(8,128)(2,1)S(1)} copy(bf16[2,128,2048]{2,0,1:T(2,128)(2,1)} %bitcast.25) | data formatting | bytes 2097152 | tf_op jit(solution)/shard_map/transpose | solution.py:205
  4.9 0.0 copy-start.4
  5.0 1.0 copy-done.4
  6.0 47.8 %shard_map.91 = (bf16[16,256,128]{2,1,0:T(8,128)(2,1)S(1)}, bf16[16,256,128]{2,1,0:T(8,128)(2,1)S(1)}, f32[16,256,128]{2,1,0:T(8,128)S(1)}) custom-call(bf16[256,2048]{1,0:T(8,128)(2,1)S(1)} %bitcast.17, bf16[256,2048]{1,0:T(8,128)(2,1)S(1)} %bitcast.18, bf16[128,2048]{1,0:T(8,128)(2,1)S(1)} %copy-done.4, f32[128,16]{1,0:T(8,128)S(1)} %copy.19.cumt_ref, ...), custom_call_target="tpu_custom_call" | custom-call | tf_op jit(solution)/shard_map/pallas_call | solution.py:209
  53.8 0.0 copy-start.1
  53.8 1.3 copy-done.1
  55.1 0.0 copy-start.2
  55.1 1.0 copy-done.2
  56.1 0.0 copy-start.3
  56.1 1.0 copy-done.3
  57.1 1.3 copy.20
  58.4 1.0 copy.21
  59.4 85.7 %shard_map.92 = bf16[128,2048]{1,0:T(8,128)(2,1)} custom-call(bf16[16,256,128]{2,1,0:T(8,128)(2,1)} %copy-done.2, bf16[16,256,128]{2,1,0:T(8,128)(2,1)} %copy-done.3, f32[16,256,128]{2,1,0:T(8,128)} %copy-done.1, bf16[16,128,128]{2,1,0:T(8,128)(2,1)} %bitcast.22, f32[1,128]{1,0:T(1,128)} %bitcast.26, bf16[4096,2048]{1,0:T(8,128)(2,1)} %w_ref.1), custom_call_target="tpu_custom_call" | custom-call | tf_op jit(solution)/shard_map/pallas_call | solution.py:228
  145.1 1.9 %copy.23 = bf16[128,2048]{1,0:T(8,128)(2,1)} copy(bf16[128,2048]{1,0:T(8,128)(2,1)} %shard_map.92) | data formatting | bytes 1048576
  (1 shorter events, 0.0 us)
Async XLA Ops:
  0.0 1.5 %copy-start = (f32[16,128]{1,0:T(8,128)S(1)}, f32[16,128]{1,0:T(8,128)}, u32[]{:S(2)}) copy-start(f32[16,128]{1,0:T(8,128)} %param.13) | copy-start | bytes 24580
  4.9 1.0 copy-start.4
  53.8 1.3 copy-start.1
  55.1 1.0 copy-start.2
  56.1 1.0 copy-start.3

commit v2 on v1

v2 whole, which is shorter than its diff:
```python
import functools

import jax
import jax.numpy as jnp
from jax import lax
from jax.experimental import pallas as pl
from jax.experimental.pallas import tpu as pltpu
from jax.sharding import PartitionSpec as P

DK = 128
NH = 2
EPS = 1e-06
F32 = jnp.float32
BF16 = jnp.bfloat16
MESH = pl.DeviceIdType.MESH
MIB = 1024 * 1024


def mm(a, b):
    return jnp.dot(a, b, preferred_element_type=F32)


def mm_t(a, b):
    return lax.dot_general(a, b, (((1,), (1,)), ((), ())), preferred_element_type=F32)


def t_mm(a, b):
    return lax.dot_general(a, b, (((0,), (0,)), ((), ())), preferred_element_type=F32)


def split(x):
    hi = x.astype(BF16)
    return hi, (x - hi.astype(F32)).astype(BF16)


def mm3(a, b):
    return mm(a[0], b[0]) + (mm(a[0], b[1]) + mm(a[1], b[0]))


def prepare(group):
    tok = group[0]["q"].shape[0]
    span = tok
    half = tok // 2
    row_at = lax.broadcasted_iota(jnp.int32, (span, span), 0)
    col_at = lax.broadcasted_iota(jnp.int32, (span, span), 1)

    def time_of(index):
        return jnp.where(index < half, 2 * index, 2 * (index - half) + 1)

    row_time, col_time = time_of(row_at), time_of(col_at)
    apart = row_time ^ col_time
    strictly = row_time > col_time
    diagonal = row_at == col_at
    unit = jnp.where(diagonal, 1.0, 0.0)
    token_at = jnp.where(col_at < half, col_at, col_at - half)
    seen = [row_at >= token_at, row_at >= token_at + half]
    blocks = [slice(0, span), slice(span, 2 * span)]

    lowers, corners, norms = [], [], []
    for x in group:
        k = [x["k"][b] for b in blocks]
        grams = [mm_t(kb, kb) for kb in k]
        cross = mm_t(k[1], k[0])
        on_diag = [jnp.where(diagonal, g, 0.0) for g in grams]
        rk_row = [lax.rsqrt(jnp.sum(d, axis=0, keepdims=True) + EPS) for d in on_diag]
        rk_col = [lax.rsqrt(jnp.sum(d, axis=1, keepdims=True) + EPS) for d in on_diag]
        cr = [x["cum_row"][:, b] for b in blocks]
        cc = [x["cum_col"][b] for b in blocks]
        sc = [x["s_col"][b] for b in blocks]
        for b in range(2):
            fade = jnp.exp(jnp.where(strictly, cc[b] - cr[b], 0.0))
            lowers.append(jnp.where(strictly, (sc[b] * rk_col[b]) * (grams[b] * fade) * rk_row[b], 0.0))
        corners.append((sc[1] * rk_col[1]) * (cross * jnp.exp(cc[1] - cr[0])) * rk_row[0])
        norms.append((rk_row, rk_col, cr, cc, sc))

    inverses = [unit - jnp.where(apart == 1, low, 0.0) for low in lowers]
    width = 2
    while width < span:
        here = (apart >= width) & (apart < 2 * width)
        rounded = [inv.astype(BF16) for inv in inverses]
        firsts = [mm(r, jnp.where(here, low, 0.0).astype(BF16)).astype(BF16) for r, low in zip(rounded, lowers)]
        inverses = [inv - mm(f, r) for inv, f, r in zip(inverses, firsts, rounded)]
        width *= 2
    parts = [split(inv) for inv in inverses]
    residuals = [unit - inv - mm3(split(low), p) for inv, low, p in zip(inverses, lowers, parts)]
    inverses = [inv + mm(p[0], r.astype(BF16)) for inv, p, r in zip(inverses, parts, residuals)]

    firsts = []
    for i, x in enumerate(group):
        rk_row, _, cr, _, _ = norms[i]
        by_value = inverses[2 * i] * x["s_row"][:, blocks[0]]
        val_hi, val_lo = split(by_value)
        key_hi, key_lo = split(by_value * (jnp.exp(cr[0]) * rk_row[0]))
        k, v = x["k"][blocks[0]], x["v"][blocks[0]]
        firsts.append(jnp.concatenate([mm(key_hi, k) + mm(key_lo, k), mm(val_hi, v) + mm(val_lo, v)], axis=1))
    first_parts = [split(f) for f in firsts]
    seconds = []
    for i, x in enumerate(group):
        _, rk_col, _, cc, sc = norms[i]
        k, v = x["k"][blocks[1]].astype(F32), x["v"][blocks[1]].astype(F32)
        right = jnp.concatenate([(sc[1] * jnp.exp(cc[1]) * rk_col[1]) * k, sc[1] * v], axis=1)
        right = right - mm3(split(corners[i]), first_parts[i])
        seconds.append(mm3(split(inverses[2 * i + 1]), split(right)))
    second_parts = [split(s) for s in seconds]

    results = []
    for i, x in enumerate(group):
        rk_row, rk_col, cr, cc, _ = norms[i]
        end = x["cum_row"][:, 2 * span - 1 :]
        ctok = x["cum_tok"]
        q = x["q"]
        qf = q.astype(F32)
        rq = lax.rsqrt(jnp.sum(qf * qf, axis=1, keepdims=True) + EPS)
        mult, add, read = 0.0, 0.0, 0.0
        for b, (whole, pieces) in enumerate([(firsts[i], first_parts[i]), (seconds[i], second_parts[i])]):
            kb = x["k"][blocks[b]]
            faded_hi, faded_lo = split((jnp.exp(end - cc[b]) * rk_col[b]) * whole)
            mult = mult - t_mm(kb, faded_hi[:, :DK])
            add = add + (t_mm(faded_hi[:, DK:], kb) + t_mm(faded_lo[:, DK:], kb))
            lag = jnp.exp(jnp.where(seen[b], ctok - cr[b], 0.0))
            weights = jnp.where(seen[b], (rq * rk_row[b]) * (lag * mm_t(q, kb)), 0.0)
            read = read + mm3(split(weights), pieces)
        query_hi, query_lo = split((jnp.exp(ctok) * rq) * qf - read[:, :DK])
        results.append((mult.astype(BF16), query_hi, query_lo, add, read[:, DK:]))
    return results


def prepare_kernel(together, k_ref, v_ref, q_ref, cumt_ref, ctok_ref, st_ref, cum_ref, s_ref, map_ref, add_ref):
    def column(ref, head):
        lane = lax.broadcasted_iota(jnp.int32, ref.shape, 1)
        return jnp.sum(jnp.where(lane == head, ref[...], 0.0), axis=1, keepdims=True)

    group = []
    for i in range(together):
        head = pl.program_id(0) * together + i
        cols = slice(i * DK, (i + 1) * DK)
        group.append(dict(
            k=k_ref[:, cols], v=v_ref[:, cols], q=q_ref[:, cols],
            cum_col=column(cumt_ref, head), cum_tok=column(ctok_ref, head), s_col=column(st_ref, head),
            cum_row=cum_ref[i], s_row=s_ref[i],
        ))
    for i, (mult, query_hi, query_lo, add, local) in enumerate(prepare(group)):
        map_ref[i, 0], map_ref[i, 1], map_ref[i, 2] = mult, query_hi, query_lo
        add_ref[i, 0], add_ref[i, 1] = add, local


def relay_kernel(
    n, heads, group, map_hbm, add_hbm, gate_ref, end_ref, gain_ref, w_ref, out_ref,
    w_vmem, maps, adds, arrived, leaving, gated, total,
    w_sem, map_sem, add_sem, send_sem, recv_sem, gsend_sem, grecv_sem,
):
    me = lax.axis_index("seq")
    core = lax.axis_index("head")
    right, left = lax.rem(me + 1, n), lax.rem(me + n - 1, n)
    other = 1 - core
    part = DK // 2

    def load_map(h):
        return pltpu.make_async_copy(map_hbm.at[h], maps.at[h], map_sem.at[h])

    def load_add(h):
        return pltpu.make_async_copy(add_hbm.at[h], adds.at[h], add_sem.at[h])

    @pl.loop(0, heads)
    def _(h):
        load_map(h).start()
        load_add(h).start()

    load = pltpu.make_async_copy(w_ref, w_vmem, w_sem)
    load.start()
    barrier = pltpu.get_barrier_semaphore()
    pl.semaphore_signal(barrier, inc=1, device_id=(left, core), device_id_type=MESH)
    pl.semaphore_signal(barrier, inc=1, device_id=(me, other), device_id_type=MESH)

    @pl.when(me == 0)
    def _():
        arrived[...] = jnp.zeros_like(arrived)

    pl.semaphore_wait(barrier, 2)

    def onward(h, i):
        return pltpu.make_async_remote_copy(
            src_ref=leaving.at[2 * h + i], dst_ref=arrived.at[2 * h + i],
            send_sem=send_sem.at[2 * h + i], recv_sem=recv_sem.at[2 * h + i],
            device_id=(right, core), device_id_type=MESH,
        )

    def across(h):
        slot = gated.at[core * heads + h]
        return pltpu.make_async_remote_copy(
            src_ref=slot, dst_ref=slot, send_sem=gsend_sem.at[h], recv_sem=grecv_sem.at[h],
            device_id=(me, other), device_id_type=MESH,
        )

    @pl.loop(0, heads)
    def _(h):
        load_map(h).wait()
        load_add(h).wait()
        end = end_ref[h]
        for i in range(2):

            @pl.when(me > 0)
            def _():
                onward(h, i).wait_recv()

            state = arrived[2 * h + i]
            moved = mm_t(state.astype(BF16), maps[h, 0])
            leaving[2 * h + i] = (end * state + adds[h, 0, i * part : (i + 1) * part]) + moved

            @pl.when(me < n - 1)
            def _():
                onward(h, i).start()

        s_hi, s_lo = split(jnp.concatenate([arrived[2 * h], arrived[2 * h + 1]], axis=0))
        rows = mm_t(maps[h, 1], s_hi) + (mm_t(maps[h, 1], s_lo) + mm_t(maps[h, 2], s_hi)) + adds[h, 1]
        scale = lax.rsqrt(jnp.mean(rows * rows, axis=1, keepdims=True) + EPS)
        x = gate_ref[:, pl.ds(pl.multiple_of(h * DK, DK), DK)].astype(F32)
        gated[core * heads + h] = (rows * scale * gain_ref[...] * (x / (1.0 + jnp.exp(-x)))).astype(BF16)
        across(h).start()

    load.wait()

    def project(base):
        block = jnp.concatenate([gated[base + i] for i in range(group)], axis=1)
        start = pl.multiple_of(base * DK, group * DK)
        return mm(block, w_vmem[pl.ds(start, group * DK), :])

    total[...] = project(core * heads)

    @pl.loop(1, heads // group)
    def _(g):
        total[...] += project(core * heads + g * group)

    @pl.loop(0, heads // group)
    def _(g):
        for i in range(group):
            across(g * group + i).wait_recv()
        total[...] += project(other * heads + g * group)

    out_ref[...] = total[...].astype(out_ref.dtype)

    @pl.loop(0, heads)
    def _(h):
        across(h).wait_send()

        @pl.when(me < n - 1)
        def _():
            onward(h, 0).wait_send()
            onward(h, 1).wait_send()


def shards(n, query, keys, values, beta, gate_log, house_count, out_gate, norm_gain, out_weight):
    tok = query.shape[0]
    heads = query.shape[1] // DK
    steps = NH * tok
    half = tok // 2
    width = out_weight.shape[1]
    active = (jnp.arange(NH, dtype=jnp.int32)[:, None] < house_count[None, :]).astype(F32)
    strength = (beta * active[:, None, :]).reshape(NH, heads, 2, half).transpose(1, 2, 0, 3).reshape(heads, steps)
    upper = (jnp.arange(tok)[:, None] <= jnp.arange(tok)[None, :]).astype(F32)
    cum = jnp.dot(gate_log, upper, precision=lax.Precision.HIGHEST)
    cum_steps = jnp.broadcast_to(cum.reshape(heads, 2, 1, half), (heads, 2, NH, half)).reshape(heads, steps)
    k2 = keys.reshape(2, half, NH, heads * DK).transpose(0, 2, 1, 3).reshape(steps, heads * DK)
    v2 = values.reshape(2, half, NH, heads * DK).transpose(0, 2, 1, 3).reshape(steps, heads * DK)
    ends = jnp.broadcast_to(jnp.exp(cum[:, tok - 1 :])[:, :, None], (heads, 1, DK))

    together = 4
    maps, adds = pl.pallas_call(
        functools.partial(prepare_kernel, together),
        grid=(heads // together,),
        in_specs=[
            pl.BlockSpec((steps, together * DK), lambda i: (0, i)),
            pl.BlockSpec((steps, together * DK), lambda i: (0, i)),
            pl.BlockSpec((tok, together * DK), lambda i: (0, i)),
            pl.BlockSpec((steps, heads), lambda i: (0, 0)),
            pl.BlockSpec((tok, heads), lambda i: (0, 0)),
            pl.BlockSpec((steps, heads), lambda i: (0, 0)),
            pl.BlockSpec((together, 1, steps), lambda i: (i, 0, 0)),
            pl.BlockSpec((together, 1, steps), lambda i: (i, 0, 0)),
        ],
        out_specs=[
            pl.BlockSpec((together, 3, tok, DK), lambda i: (i, 0, 0, 0)),
            pl.BlockSpec((together, 2, tok, DK), lambda i: (i, 0, 0, 0)),
        ],
        out_shape=[
            jax.ShapeDtypeStruct((heads, 3, tok, DK), BF16),
            jax.ShapeDtypeStruct((heads, 2, tok, DK), F32),
        ],
        compiler_params=pltpu.CompilerParams(vmem_limit_bytes=40 * MIB),
    )(k2, v2, query, cum_steps.T, cum.T, strength.T, cum_steps[:, None, :], strength[:, None, :])

    group = 4
    vmem = pl.BlockSpec(memory_space=pltpu.VMEM)
    hbm = pl.BlockSpec(memory_space=pl.ANY)
    return pl.pallas_call(
        functools.partial(relay_kernel, n, heads, group),
        in_specs=[hbm, hbm, vmem, vmem, vmem, hbm],
        out_specs=vmem,
        out_shape=jax.ShapeDtypeStruct((tok, width), BF16),
        scratch_shapes=[
            pltpu.VMEM(out_weight.shape, BF16),
            pltpu.VMEM((heads, 3, tok, DK), BF16),
            pltpu.VMEM((heads, 2, tok, DK), F32),
            pltpu.VMEM((2 * heads, DK // 2, DK), F32),
            pltpu.VMEM((2 * heads, DK // 2, DK), F32),
            pltpu.VMEM((2 * heads, tok, DK), BF16),
            pltpu.VMEM((tok, width), F32),
            pltpu.SemaphoreType.DMA,
            pltpu.SemaphoreType.DMA((heads,)),
            pltpu.SemaphoreType.DMA((heads,)),
            pltpu.SemaphoreType.DMA((2 * heads,)),
            pltpu.SemaphoreType.DMA((2 * heads,)),
            pltpu.SemaphoreType.DMA((heads,)),
            pltpu.SemaphoreType.DMA((heads,)),
        ],
        compiler_params=pltpu.CompilerParams(
            collective_id=0, has_side_effects=True, vmem_limit_bytes=56 * MIB
        ),
    )(maps, adds, out_gate, ends, norm_gain[None, :], out_weight)


def solution(mesh):
    return jax.shard_map(
        functools.partial(shards, mesh.shape["seq"]),
        mesh=mesh,
        in_specs=(
            P("seq", "head"),
            P("seq", None, "head"),
            P("seq", None, "head"),
            P(None, "head", "seq"),
            P("head", "seq"),
            P("seq"),
            P("seq", "head"),
            P(),
            P(None, "head"),
        ),
        out_specs=P("seq", "head"),
        check_vma=False,
    )
```

time: 149 us -> 106 us (0.71); the launches traced: 147 us -> 106 us
  Pallas kernels: 133 us -> 96.2 us
  local copies, waits for them, and re-layouts: 11.9 us -> 7.96 us
    pallas_call x1, Pallas kernels: 47.8 us -> 18.1 us  [shards(): pl.pallas_call(functools.partial(prepare_kernel, together), grid=(heads /...]
    pallas_call x1, Pallas kernels: 85.7 us -> 78.1 us  [shards(): pl.pallas_call(functools.partial(relay_kernel, n, heads, group), in_specs...]
    transpose x4 -> x1, local copies, waits for them, and re-layouts: 3.27 us -> 0.1 us  [shards(): (beta * active[:, None, :]).reshape(NH, heads, 2, half)]
    unnamed x12, local copies, waits for them, and re-layouts: 7.53 us -> 4.46 us
where the time goes in v2:
time: 106 us
  Pallas kernels  96.2 us (91%)
  local copies, waits for them, and re-layouts  7.96 us (8%)
  other arithmetic  1.47 us (1%)
    pallas_call x1, Pallas kernels, shards(): pl.pallas_call(functools.partial(relay_kernel, n, heads, group), in_specs...  78.1 us
    pallas_call x1, Pallas kernels, shards(): pl.pallas_call(functools.partial(prepare_kernel, together), grid=(heads /...  18.1 us
    unnamed x12, local copies, waits for them, and re-layouts  4.46 us

profile of v2, /device:TPU:30, one launch (start us, length us, event | category | flops | bytes accessed | tf_op | source)
XLA Modules:
  0.0 105.9 jit_solution(16379252928369560110)
XLA Ops:
  0.0 0.0 copy-start
  0.0 0.0 copy-start.4
  0.0 0.7 compare_convert_fusion
  0.8 0.0 copy-done
  0.8 0.1 fusion
  0.9 0.2 fusion.1
  1.1 0.7 broadcast_in_dim.26.end_ref
  1.8 0.7 broadcast_multiply_fusion
  2.5 0.1 reshape.49
  2.6 0.1 broadcast_in_dim.10
  2.7 0.1 broadcast_in_dim_reshape.6.cum_ref
  2.8 0.1 broadcast_in_dim_reshape.7.s_ref
  2.9 0.1 copy.23
  3.0 0.1 copy.21.ctok_ref
  3.1 0.1 copy.20
  3.3 0.0 copy-start.3
  3.3 1.6 %copy.16 = bf16[2,64,2,2048]{3,1,2,0:T(8,128)(2,1)S(1)} copy(bf16[2,64,2,2048]{3,2,1,0:T(2,128)(2,1)} %bitcast.25) | data formatting | bytes 2097152 | tf_op jit(solution)/shard_map/reshape | solution.py:263
  4.9 0.0 copy-done.4
  4.9 0.4 copy.17
  5.3 0.0 copy-done.3
  5.3 18.1 %shard_map.91 = (bf16[16,3,128,128]{3,2,1,0:T(8,128)(2,1)S(1)}, f32[16,2,128,128]{3,2,1,0:T(8,128)S(1)}) custom-call(bf16[256,2048]{1,0:T(8,128)(2,1)S(1)} %bitcast.21, bf16[256,2048]{1,0:T(8,128)(2,1)S(1)} %bitcast.22, bf16[128,2048]{1,0:T(8,128)(2,1)S(1)} %copy-done.3, f32[256,16]{1,0:T(8,128)S(1)} %bitcast.24, f32[128,16]{1,0:T(8,128)S(1)} %copy.21.ctok_ref, ...), custom_call_target="tpu_custom_call" | custom-call | tf_op jit(solution)/shard_map/pallas_call | solution.py:268
  23.4 0.0 copy-start.1
  23.5 1.3 %copy-done.1 = f32[16,2,128,128]{3,2,1,0:T(8,128)} copy-done((f32[16,2,128,128]{3,2,1,0:T(8,128)}, f32[16,2,128,128]{3,2,1,0:T(8,128)S(1)}, u32[]{:S(2)}) %copy-start.1) | copy-done | bytes 2097176
  24.8 0.0 copy-start.2
  24.8 1.1 %copy-done.2 = bf16[16,3,128,128]{3,2,1,0:T(8,128)(2,1)} copy-done((bf16[16,3,128,128]{3,2,1,0:T(8,128)(2,1)}, bf16[16,3,128,128]{3,2,1,0:T(8,128)(2,1)S(1)}, u32[]{:S(2)}) %copy-start.2) | copy-done | bytes 1572888
  25.9 78.1 %shard_map.92 = bf16[128,2048]{1,0:T(8,128)(2,1)} custom-call(bf16[16,3,128,128]{3,2,1,0:T(8,128)(2,1)} %copy-done.2, f32[16,2,128,128]{3,2,1,0:T(8,128)} %copy-done.1, bf16[128,2048]{1,0:T(8,128)(2,1)} %gate_ref.1, f32[16,1,128]{2,1,0:T(1,128)} %broadcast_in_dim.26.end_ref, f32[1,128]{1,0:T(1,128)} %bitcast.31, bf16[4096,2048]{1,0:T(8,128)(2,1)} %w_ref.1), custom_call_target="tpu_custom_call" | custom-call | tf_op jit(solution)/shard_map/pallas_call | solution.py:295
  104.0 1.9 %copy.27 = bf16[128,2048]{1,0:T(8,128)(2,1)} copy(bf16[128,2048]{1,0:T(8,128)(2,1)} %shard_map.92) | data formatting | bytes 1048576
  (3 shorter events, 0.1 us)
Async XLA Ops:
  0.0 0.8 copy-start
  0.0 4.9 %copy-start.4 = (bf16[128,2,2048]{2,1,0:T(2,128)(2,1)S(1)}, bf16[128,2,2048]{2,1,0:T(2,128)(2,1)}, u32[]{:S(2)}) copy-start(bf16[128,2,2048]{2,1,0:T(2,128)(2,1)} %param.11) | copy-start | bytes 3145732
  3.3 2.0 %copy-start.3 = (bf16[128,2048]{1,0:T(8,128)(2,1)S(1)}, bf16[128,2048]{1,0:T(8,128)(2,1)}, u32[]{:S(2)}) copy-start(bf16[128,2048]{1,0:T(8,128)(2,1)} %q_ref.1) | copy-start | bytes 1572868
  23.4 1.3 %copy-start.1 = (f32[16,2,128,128]{3,2,1,0:T(8,128)}, f32[16,2,128,128]{3,2,1,0:T(8,128)S(1)}, u32[]{:S(2)}) copy-start(f32[16,2,128,128]{3,2,1,0:T(8,128)S(1)} %get-tuple-element.8.add_hbm) | copy-start | bytes 6291460
  24.8 1.1 %copy-start.2 = (bf16[16,3,128,128]{3,2,1,0:T(8,128)(2,1)}, bf16[16,3,128,128]{3,2,1,0:T(8,128)(2,1)S(1)}, u32[]{:S(2)}) copy-start(bf16[16,3,128,128]{3,2,1,0:T(8,128)(2,1)S(1)} %get-tuple-element.7.map_hbm) | copy-start | bytes 4718596

commit v3 on v2

--- a/solution.py
+++ b/solution.py
@@ -121,7 +121,7 @@
             weights = jnp.where(seen[b], (rq * rk_row[b]) * (lag * mm_t(q, kb)), 0.0)
             read = read + mm3(split(weights), pieces)
         query_hi, query_lo = split((jnp.exp(ctok) * rq) * qf - read[:, :DK])
-        results.append((mult.astype(BF16), query_hi, query_lo, add, read[:, DK:]))
+        results.append((mult.astype(BF16), add.astype(BF16), query_hi, query_lo, add, read[:, DK:]))
     return results
 
 
@@ -139,21 +139,26 @@
             cum_col=column(cumt_ref, head), cum_tok=column(ctok_ref, head), s_col=column(st_ref, head),
             cum_row=cum_ref[i], s_row=s_ref[i],
         ))
-    for i, (mult, query_hi, query_lo, add, local) in enumerate(prepare(group)):
-        map_ref[i, 0], map_ref[i, 1], map_ref[i, 2] = mult, query_hi, query_lo
+    for i, (mult, add_low, query_hi, query_lo, add, local) in enumerate(prepare(group)):
+        map_ref[i, 0], map_ref[i, 1] = mult, add_low
+        map_ref[i, 2], map_ref[i, 3] = query_hi, query_lo
         add_ref[i, 0], add_ref[i, 1] = add, local
 
 
 def relay_kernel(
     n, heads, group, map_hbm, add_hbm, gate_ref, end_ref, gain_ref, w_ref, out_ref,
-    w_vmem, maps, adds, arrived, leaving, gated, total,
-    w_sem, map_sem, add_sem, send_sem, recv_sem, gsend_sem, grecv_sem,
+    w_vmem, maps, adds, mates, mate_end, joint_map, joint_add, arrived, leaving, own, gated, total,
+    w_sem, map_sem, add_sem, end_sem, mate_send, mate_recv, send_sem, recv_sem, gsend_sem, grecv_sem,
 ):
     me = lax.axis_index("seq")
     core = lax.axis_index("head")
-    right, left = lax.rem(me + 1, n), lax.rem(me + n - 1, n)
+    odd = lax.rem(me, 2)
+    first = me - odd
+    mate = me + 1 - 2 * odd
+    after, before = lax.rem(first + 2, n), lax.rem(first + n - 2, n)
     other = 1 - core
     part = DK // 2
+    relays = (odd == 0) & (me < n - 2)
 
     def load_map(h):
         return pltpu.make_async_copy(map_hbm.at[h], maps.at[h], map_sem.at[h])
@@ -161,28 +166,23 @@
     def load_add(h):
         return pltpu.make_async_copy(add_hbm.at[h], adds.at[h], add_sem.at[h])
 
-    @pl.loop(0, heads)
-    def _(h):
-        load_map(h).start()
-        load_add(h).start()
-
-    load = pltpu.make_async_copy(w_ref, w_vmem, w_sem)
-    load.start()
-    barrier = pltpu.get_barrier_semaphore()
-    pl.semaphore_signal(barrier, inc=1, device_id=(left, core), device_id_type=MESH)
-    pl.semaphore_signal(barrier, inc=1, device_id=(me, other), device_id_type=MESH)
-
-    @pl.when(me == 0)
-    def _():
-        arrived[...] = jnp.zeros_like(arrived)
-
-    pl.semaphore_wait(barrier, 2)
-
-    def onward(h, i):
+    def swap_end():
+        return pltpu.make_async_remote_copy(
+            src_ref=end_ref, dst_ref=mate_end, send_sem=end_sem.at[0], recv_sem=end_sem.at[1],
+            device_id=(mate, core), device_id_type=MESH,
+        )
+
+    def swap(h):
+        return pltpu.make_async_remote_copy(
+            src_ref=map_hbm.at[h, pl.ds(0, 2)], dst_ref=mates.at[h], send_sem=mate_send.at[h], recv_sem=mate_recv.at[h],
+            device_id=(mate, core), device_id_type=MESH,
+        )
+
+    def onward(h, i, to):
         return pltpu.make_async_remote_copy(
             src_ref=leaving.at[2 * h + i], dst_ref=arrived.at[2 * h + i],
-            send_sem=send_sem.at[2 * h + i], recv_sem=recv_sem.at[2 * h + i],
-            device_id=(right, core), device_id_type=MESH,
+            send_sem=send_sem.at[to, 2 * h + i], recv_sem=recv_sem.at[2 * h + i],
+            device_id=(after + to, core), device_id_type=MESH,
         )
 
     def across(h):
@@ -192,27 +192,82 @@
             device_id=(me, other), device_id_type=MESH,
         )
 
+    barrier = pltpu.get_barrier_semaphore()
+    pl.semaphore_signal(barrier, inc=1, device_id=(mate, core), device_id_type=MESH)
+    pl.semaphore_signal(barrier, inc=1, device_id=(me, other), device_id_type=MESH)
+    pl.semaphore_signal(barrier, inc=1, device_id=(before, core), device_id_type=MESH)
+
     @pl.loop(0, heads)
     def _(h):
+        load_map(h).start()
+        load_add(h).start()
+
+    @pl.when(me < 2)
+    def _():
+        arrived[...] = jnp.zeros_like(arrived)
+
+    pl.semaphore_wait(barrier, 4 - 2 * odd)
+    swap_end().start()
+
+    @pl.loop(0, heads)
+    def _(h):
+        swap(h).start()
+
+    load = pltpu.make_async_copy(w_ref, w_vmem, w_sem)
+    load.start()
+
+    def ready(h):
         load_map(h).wait()
         load_add(h).wait()
-        end = end_ref[h]
+        swap(h).wait_recv()
+
+    def join(h):
+        mine, theirs = maps[h, 0], mates[h, 0]
+        mine_end, theirs_end = end_ref[h], mate_end[h]
+        add = adds[h, 0]
+        joint_map[h] = (
+            theirs_end * mine.astype(F32) + mine_end * theirs.astype(F32) + mm(theirs, mine)
+        ).astype(BF16)
+        joint_add[h] = theirs_end * add + mm_t(add.astype(BF16), theirs) + mates[h, 1].astype(F32)
+
+    swap_end().wait_recv()
+    ready(0)
+    join(0)
+
+    @pl.loop(0, heads)
+    def _(h):
         for i in range(2):
 
-            @pl.when(me > 0)
+            @pl.when(me > 1)
             def _():
-                onward(h, i).wait_recv()
-
-            state = arrived[2 * h + i]
-            moved = mm_t(state.astype(BF16), maps[h, 0])
-            leaving[2 * h + i] = (end * state + adds[h, 0, i * part : (i + 1) * part]) + moved
-
-            @pl.when(me < n - 1)
+                onward(h, i, 0).wait_recv()
+
+            @pl.when(relays)
             def _():
-                onward(h, i).start()
-
-        s_hi, s_lo = split(jnp.concatenate([arrived[2 * h], arrived[2 * h + 1]], axis=0))
-        rows = mm_t(maps[h, 1], s_hi) + (mm_t(maps[h, 1], s_lo) + mm_t(maps[h, 2], s_hi)) + adds[h, 1]
+                state = arrived[2 * h + i]
+                moved = mm_t(state.astype(BF16), joint_map[h])
+                end = end_ref[h] * mate_end[h]
+                leaving[2 * h + i] = (end * state + joint_add[h, i * part : (i + 1) * part]) + moved
+                onward(h, i, 0).start()
+                onward(h, i, 1).start()
+
+        @pl.when(odd == 0)
+        def _():
+            own[:part] = arrived[2 * h]
+            own[part:] = arrived[2 * h + 1]
+
+        @pl.when(odd == 1)
+        def _():
+            state = jnp.concatenate([arrived[2 * h], arrived[2 * h + 1]], axis=0)
+            own[...] = mate_end[h] * state + mm_t(state.astype(BF16), mates[h, 0]) + mates[h, 1].astype(F32)
+
+        @pl.when(h < heads - 1)
+        def _():
+            ready(h + 1)
+
+        join(lax.rem(h + 1, heads))
+        s_hi, s_lo = split(own[...])
+        rows = mm_t(maps[h, 2], s_hi) + (mm_t(maps[h, 2], s_lo) + mm_t(maps[h, 3], s_hi)) + adds[h, 1]
         scale = lax.rsqrt(jnp.mean(rows * rows, axis=1, keepdims=True) + EPS)
         x = gate_ref[:, pl.ds(pl.multiple_of(h * DK, DK), DK)].astype(F32)
         gated[core * heads + h] = (rows * scale * gain_ref[...] * (x / (1.0 + jnp.exp(-x)))).astype(BF16)
@@ -242,11 +297,15 @@
     @pl.loop(0, heads)
     def _(h):
         across(h).wait_send()
-
-        @pl.when(me < n - 1)
+        swap(h).wait_send()
+
+        @pl.when(relays)
         def _():
-            onward(h, 0).wait_send()
-            onward(h, 1).wait_send()
+            for i in range(2):
+                onward(h, i, 0).wait_send()
+                onward(h, i, 1).wait_send()
+
+    swap_end().wait_send()
 
 
 def shards(n, query, keys, values, beta, gate_log, house_count, out_gate, norm_gain, out_weight):
@@ -279,19 +338,19 @@
             pl.BlockSpec((together, 1, steps), lambda i: (i, 0, 0)),
         ],
         out_specs=[
-            pl.BlockSpec((together, 3, tok, DK), lambda i: (i, 0, 0, 0)),
+            pl.BlockSpec((together, 4, tok, DK), lambda i: (i, 0, 0, 0)),
             pl.BlockSpec((together, 2, tok, DK), lambda i: (i, 0, 0, 0)),
         ],
         out_shape=[
-            jax.ShapeDtypeStruct((heads, 3, tok, DK), BF16),
+            jax.ShapeDtypeStruct((heads, 4, tok, DK), BF16),
             jax.ShapeDtypeStruct((heads, 2, tok, DK), F32),
         ],
-        compiler_params=pltpu.CompilerParams(vmem_limit_bytes=40 * MIB),
+        compiler_params=pltpu.CompilerParams(vmem_limit_bytes=61 * MIB),
     )(k2, v2, query, cum_steps.T, cum.T, strength.T, cum_steps[:, None, :], strength[:, None, :])
 
     group = 4
     vmem = pl.BlockSpec(memory_space=pltpu.VMEM)
-    hbm = pl.BlockSpec(memory_space=pl.ANY)
+    hbm = pl.BlockSpec(memory_space=pltpu.HBM)
     return pl.pallas_call(
         functools.partial(relay_kernel, n, heads, group),
         in_specs=[hbm, hbm, vmem, vmem, vmem, hbm],
@@ -299,16 +358,24 @@
         out_shape=jax.ShapeDtypeStruct((tok, width), BF16),
         scratch_shapes=[
             pltpu.VMEM(out_weight.shape, BF16),
-            pltpu.VMEM((heads, 3, tok, DK), BF16),
+            pltpu.VMEM((heads, 4, tok, DK), BF16),
             pltpu.VMEM((heads, 2, tok, DK), F32),
+            pltpu.VMEM((heads, 2, DK, DK), BF16),
+            pltpu.VMEM(ends.shape, F32),
+            pltpu.VMEM((heads, DK, DK), BF16),
+            pltpu.VMEM((heads, DK, DK), F32),
             pltpu.VMEM((2 * heads, DK // 2, DK), F32),
             pltpu.VMEM((2 * heads, DK // 2, DK), F32),
+            pltpu.VMEM((DK, DK), F32),
             pltpu.VMEM((2 * heads, tok, DK), BF16),
             pltpu.VMEM((tok, width), F32),
             pltpu.SemaphoreType.DMA,
             pltpu.SemaphoreType.DMA((heads,)),
             pltpu.SemaphoreType.DMA((heads,)),
-            pltpu.SemaphoreType.DMA((2 * heads,)),
+            pltpu.SemaphoreType.DMA((2,)),
+            pltpu.SemaphoreType.DMA((heads,)),
+            pltpu.SemaphoreType.DMA((heads,)),
+            pltpu.SemaphoreType.DMA((2, 2 * heads)),
             pltpu.SemaphoreType.DMA((2 * heads,)),
             pltpu.SemaphoreType.DMA((heads,)),
             pltpu.SemaphoreType.DMA((heads,)),

time: 106 us -> 109 us (1.028)
  local copies, waits for them, and re-layouts: 7.96 us -> 10.5 us
    unnamed x12 -> x6, local copies, waits for them, and re-layouts: 4.46 us -> 1.98 us
    pallas_call x1, Pallas kernels: 18.1 us -> 20.1 us  [shards(): pl.pallas_call(functools.partial(prepare_kernel, together), grid=(heads /...]
    pallas_call x1, Pallas kernels: 78.1 us -> 76.4 us  [shards(): pl.pallas_call(functools.partial(relay_kernel, n, heads, group), in_specs...]
where the time goes in v3:
time: 109 us
  Pallas kernels  96.6 us (89%)
  local copies, waits for them, and re-layouts  10.5 us (10%)
  other arithmetic  1.47 us (1%)
    pallas_call x1, Pallas kernels, shards(): pl.pallas_call(functools.partial(relay_kernel, n, heads, group), in_specs...  76.4 us
    pallas_call x1, Pallas kernels, shards(): pl.pallas_call(functools.partial(prepare_kernel, together), grid=(heads /...  20.1 us
    reshape x1, local copies, waits for them, and re-layouts, shards(): keys.reshape(2, half, NH, heads * DK).transpose(0, 2, 1, 3)  2.55 us

profile of v3, /device:TPU:30, one launch (start us, length us, event | category | flops | bytes accessed | tf_op | source)
XLA Modules:
  0.0 108.7 jit_solution(7979651104954908720)
XLA Ops:
  0.0 0.0 copy-start
  0.0 0.0 copy-start.1
  0.0 0.7 compare_convert_fusion
  0.8 0.0 copy-done
  0.8 0.1 fusion
  0.9 0.2 fusion.1
  1.1 0.7 broadcast_in_dim.26.end_ref
  1.8 0.7 broadcast_multiply_fusion
  2.5 0.1 reshape.49
  2.6 0.1 broadcast_in_dim.10
  2.7 0.7 broadcast_in_dim_reshape.6.cum_ref
  3.4 0.7 broadcast_in_dim_reshape.7.s_ref
  4.1 0.1 copy.23
  4.2 0.7 broadcast_in_dim.11.clone
  4.9 0.7 copy.21.ctok_ref
  5.6 0.8 copy.20
  6.4 2.5 %copy.16 = bf16[2,64,2,2048]{3,1,2,0:T(8,128)(2,1)} copy(bf16[2,64,2,2048]{3,2,1,0:T(2,128)(2,1)} %bitcast.23) | data formatting | bytes 2097152 | tf_op jit(solution)/shard_map/reshape | solution.py:322
  8.9 0.0 copy-done.1
  8.9 1.4 %copy.17 = bf16[2,64,2,2048]{3,1,2,0:T(8,128)(2,1)} copy(bf16[2,64,2,2048]{3,2,1,0:T(2,128)(2,1)S(1)} %bitcast.24) | data formatting | bytes 2097152 | tf_op jit(solution)/shard_map/reshape | solution.py:323
  10.3 20.1 %shard_map.91 = (bf16[16,4,128,128]{3,2,1,0:T(8,128)(2,1)}, f32[16,2,128,128]{3,2,1,0:T(8,128)}) custom-call(bf16[256,2048]{1,0:T(8,128)(2,1)} %bitcast.21, bf16[256,2048]{1,0:T(8,128)(2,1)} %bitcast.22, bf16[128,2048]{1,0:T(8,128)(2,1)} %q_ref.1, f32[256,16]{1,0:T(8,128)} %bitcast.26, f32[128,16]{1,0:T(8,128)} %copy.21.ctok_ref, f32[256,16]{1,0:T(8,128)} %bitcast.25, ...), custom_call_target="tpu_custom_call" | custom-call | tf_op jit(solution)/shard_map/pallas_call | solution.py:327
  30.4 76.4 %shard_map.92 = bf16[128,2048]{1,0:T(8,128)(2,1)} custom-call(bf16[16,4,128,128]{3,2,1,0:T(8,128)(2,1)} %get-tuple-element.7.map_hbm, f32[16,2,128,128]{3,2,1,0:T(8,128)} %get-tuple-element.8.add_hbm, bf16[128,2048]{1,0:T(8,128)(2,1)} %gate_ref.1, f32[16,1,128]{2,1,0:T(1,128)} %broadcast_in_dim.26.end_ref, f32[1,128]{1,0:T(1,128)} %bitcast.31, ...), custom_call_target="tpu_custom_call" | custom-call | tf_op jit(solution)/shard_map/pallas_call | solution.py:354
  106.8 1.9 %copy.27 = bf16[128,2048]{1,0:T(8,128)(2,1)} copy(bf16[128,2048]{1,0:T(8,128)(2,1)} %shard_map.92) | data formatting | bytes 1048576
  (2 shorter events, 0.0 us)
Async XLA Ops:
  0.0 0.8 copy-start
  0.0 8.9 %copy-start.1 = (bf16[128,2,2048]{2,1,0:T(2,128)(2,1)S(1)}, bf16[128,2,2048]{2,1,0:T(2,128)(2,1)}, u32[]{:S(2)}) copy-start(bf16[128,2,2048]{2,1,0:T(2,128)(2,1)} %param.11) | copy-start | bytes 3145732

commit v4 on v3

--- a/solution.py
+++ b/solution.py
@@ -147,8 +147,8 @@
 
 def relay_kernel(
     n, heads, group, map_hbm, add_hbm, gate_ref, end_ref, gain_ref, w_ref, out_ref,
-    w_vmem, maps, adds, mates, mate_end, joint_map, joint_add, arrived, leaving, own, gated, total,
-    w_sem, map_sem, add_sem, end_sem, mate_send, mate_recv, send_sem, recv_sem, gsend_sem, grecv_sem,
+    w_vmem, maps, adds, mates, mate_end, joint_map, joint_add, arrived, leaving, passing, gated, total,
+    w_sem, map_sem, add_sem, end_sem, mate_send, mate_recv, send_sem, pass_sem, recv_sem, gsend_sem, grecv_sem,
 ):
     me = lax.axis_index("seq")
     core = lax.axis_index("head")
@@ -178,11 +178,18 @@
             device_id=(mate, core), device_id_type=MESH,
         )
 
-    def onward(h, i, to):
+    def onward(h, i):
         return pltpu.make_async_remote_copy(
             src_ref=leaving.at[2 * h + i], dst_ref=arrived.at[2 * h + i],
-            send_sem=send_sem.at[to, 2 * h + i], recv_sem=recv_sem.at[2 * h + i],
-            device_id=(after + to, core), device_id_type=MESH,
+            send_sem=send_sem.at[2 * h + i], recv_sem=recv_sem.at[2 * h + i],
+            device_id=(after, core), device_id_type=MESH,
+        )
+
+    def sideways(h, i):
+        return pltpu.make_async_remote_copy(
+            src_ref=passing.at[2 * h + i], dst_ref=arrived.at[2 * h + i],
+            send_sem=pass_sem.at[2 * h + i], recv_sem=recv_sem.at[2 * h + i],
+            device_id=(mate, core), device_id_type=MESH,
         )
 
     def across(h):
@@ -195,23 +202,29 @@
     barrier = pltpu.get_barrier_semaphore()
     pl.semaphore_signal(barrier, inc=1, device_id=(mate, core), device_id_type=MESH)
     pl.semaphore_signal(barrier, inc=1, device_id=(me, other), device_id_type=MESH)
-    pl.semaphore_signal(barrier, inc=1, device_id=(before, core), device_id_type=MESH)
+
+    @pl.when(odd == 0)
+    def _():
+        pl.semaphore_signal(barrier, inc=1, device_id=(before, core), device_id_type=MESH)
 
     @pl.loop(0, heads)
     def _(h):
         load_map(h).start()
         load_add(h).start()
 
-    @pl.when(me < 2)
+    @pl.when(me == 0)
     def _():
         arrived[...] = jnp.zeros_like(arrived)
 
-    pl.semaphore_wait(barrier, 4 - 2 * odd)
-    swap_end().start()
-
-    @pl.loop(0, heads)
-    def _(h):
-        swap(h).start()
+    pl.semaphore_wait(barrier, 3 - odd)
+
+    @pl.when(odd == 1)
+    def _():
+        swap_end().start()
+
+        @pl.loop(0, heads)
+        def _(h):
+            swap(h).start()
 
     load = pltpu.make_async_copy(w_ref, w_vmem, w_sem)
     load.start()
@@ -219,7 +232,10 @@
     def ready(h):
         load_map(h).wait()
         load_add(h).wait()
-        swap(h).wait_recv()
+
+        @pl.when(odd == 0)
+        def _():
+            swap(h).wait_recv()
 
     def join(h):
         mine, theirs = maps[h, 0], mates[h, 0]
@@ -230,17 +246,20 @@
         ).astype(BF16)
         joint_add[h] = theirs_end * add + mm_t(add.astype(BF16), theirs) + mates[h, 1].astype(F32)
 
-    swap_end().wait_recv()
     ready(0)
-    join(0)
+
+    @pl.when(odd == 0)
+    def _():
+        swap_end().wait_recv()
+        join(0)
 
     @pl.loop(0, heads)
     def _(h):
         for i in range(2):
 
-            @pl.when(me > 1)
+            @pl.when(me > 0)
             def _():
-                onward(h, i, 0).wait_recv()
+                onward(h, i).wait_recv()
 
             @pl.when(relays)
             def _():
@@ -248,25 +267,22 @@
                 moved = mm_t(state.astype(BF16), joint_map[h])
                 end = end_ref[h] * mate_end[h]
                 leaving[2 * h + i] = (end * state + joint_add[h, i * part : (i + 1) * part]) + moved
-                onward(h, i, 0).start()
-                onward(h, i, 1).start()
+                onward(h, i).start()
+
+        @pl.when(h < heads - 1)
+        def _():
+            ready(h + 1)
 
         @pl.when(odd == 0)
         def _():
-            own[:part] = arrived[2 * h]
-            own[part:] = arrived[2 * h + 1]
-
-        @pl.when(odd == 1)
-        def _():
-            state = jnp.concatenate([arrived[2 * h], arrived[2 * h + 1]], axis=0)
-            own[...] = mate_end[h] * state + mm_t(state.astype(BF16), mates[h, 0]) + mates[h, 1].astype(F32)
-
-        @pl.when(h < heads - 1)
-        def _():
-            ready(h + 1)
-
-        join(lax.rem(h + 1, heads))
-        s_hi, s_lo = split(own[...])
+            for i in range(2):
+                state = arrived[2 * h + i]
+                moved = mm_t(state.astype(BF16), maps[h, 0])
+                passing[2 * h + i] = (end_ref[h] * state + adds[h, 0, i * part : (i + 1) * part]) + moved
+                sideways(h, i).start()
+            join(lax.rem(h + 1, heads))
+
+        s_hi, s_lo = split(jnp.concatenate([arrived[2 * h], arrived[2 * h + 1]], axis=0))
         rows = mm_t(maps[h, 2], s_hi) + (mm_t(maps[h, 2], s_lo) + mm_t(maps[h, 3], s_hi)) + adds[h, 1]
         scale = lax.rsqrt(jnp.mean(rows * rows, axis=1, keepdims=True) + EPS)
         x = gate_ref[:, pl.ds(pl.multiple_of(h * DK, DK), DK)].astype(F32)
@@ -297,15 +313,24 @@
     @pl.loop(0, heads)
     def _(h):
         across(h).wait_send()
-        swap(h).wait_send()
+
+        @pl.when(odd == 1)
+        def _():
+            swap(h).wait_send()
+
+        @pl.when(odd == 0)
+        def _():
+            sideways(h, 0).wait_send()
+            sideways(h, 1).wait_send()
 
         @pl.when(relays)
         def _():
-            for i in range(2):
-                onward(h, i, 0).wait_send()
-                onward(h, i, 1).wait_send()
-
-    swap_end().wait_send()
+            onward(h, 0).wait_send()
+            onward(h, 1).wait_send()
+
+    @pl.when(odd == 1)
+    def _():
+        swap_end().wait_send()
 
 
 def shards(n, query, keys, values, beta, gate_log, house_count, out_gate, norm_gain, out_weight):
@@ -345,7 +370,7 @@
             jax.ShapeDtypeStruct((heads, 4, tok, DK), BF16),
             jax.ShapeDtypeStruct((heads, 2, tok, DK), F32),
         ],
-        compiler_params=pltpu.CompilerParams(vmem_limit_bytes=61 * MIB),
+        compiler_params=pltpu.CompilerParams(vmem_limit_bytes=40 * MIB),
     )(k2, v2, query, cum_steps.T, cum.T, strength.T, cum_steps[:, None, :], strength[:, None, :])
 
     group = 4
@@ -366,7 +391,7 @@
             pltpu.VMEM((heads, DK, DK), F32),
             pltpu.VMEM((2 * heads, DK // 2, DK), F32),
             pltpu.VMEM((2 * heads, DK // 2, DK), F32),
-            pltpu.VMEM((DK, DK), F32),
+            pltpu.VMEM((2 * heads, DK // 2, DK), F32),
             pltpu.VMEM((2 * heads, tok, DK), BF16),
             pltpu.VMEM((tok, width), F32),
             pltpu.SemaphoreType.DMA,
@@ -375,7 +400,8 @@
             pltpu.SemaphoreType.DMA((2,)),
             pltpu.SemaphoreType.DMA((heads,)),
             pltpu.SemaphoreType.DMA((heads,)),
-            pltpu.SemaphoreType.DMA((2, 2 * heads)),
+            pltpu.SemaphoreType.DMA((2 * heads,)),
+            pltpu.SemaphoreType.DMA((2 * heads,)),
             pltpu.SemaphoreType.DMA((2 * heads,)),
             pltpu.SemaphoreType.DMA((heads,)),
             pltpu.SemaphoreType.DMA((heads,)),

time: 109 us -> 88 us (0.81)
  Pallas kernels: 96.6 us -> 77.9 us
  local copies, waits for them, and re-layouts: 10.5 us -> 8.13 us
    pallas_call x1, Pallas kernels: 76.4 us -> 59.7 us  [shards(): pl.pallas_call(functools.partial(relay_kernel, n, heads, group), in_specs...]
    unnamed x6 -> x12, local copies, waits for them, and re-layouts: 1.98 us -> 4.62 us
    pallas_call x1, Pallas kernels: 20.1 us -> 18.2 us  [shards(): pl.pallas_call(functools.partial(prepare_kernel, together), grid=(heads /...]
where the time goes in v4:
time: 88 us; the launch traced here: 87.7 us
  Pallas kernels  77.9 us (89%)
  local copies, waits for them, and re-layouts  8.13 us (9%)
  other arithmetic  1.47 us (2%)
    pallas_call x1, Pallas kernels, shards(): pl.pallas_call(functools.partial(relay_kernel, n, heads, group), in_specs...  59.7 us
    pallas_call x1, Pallas kernels, shards(): pl.pallas_call(functools.partial(prepare_kernel, together), grid=(heads /...  18.2 us
    unnamed x12, local copies, waits for them, and re-layouts  4.62 us

profile of v4, /device:TPU:30, one launch (start us, length us, event | category | flops | bytes accessed | tf_op | source)
XLA Modules:
  0.0 87.7 jit_solution(3696574506616125089)
XLA Ops:
  0.0 0.0 copy-start
  0.0 0.0 copy-start.4
  0.0 0.7 compare_convert_fusion
  0.8 0.0 copy-done
  0.8 0.1 fusion
  0.9 0.2 fusion.1
  1.1 0.7 broadcast_in_dim.26.end_ref
  1.8 0.7 broadcast_multiply_fusion
  2.5 0.1 reshape.49
  2.6 0.1 broadcast_in_dim.10
  2.7 0.1 broadcast_in_dim_reshape.6.cum_ref
  2.8 0.1 broadcast_in_dim_reshape.7.s_ref
  2.9 0.1 copy.23
  3.0 0.1 copy.21.ctok_ref
  3.1 0.1 copy.20
  3.3 0.0 copy-start.3
  3.3 1.6 %copy.16 = bf16[2,64,2,2048]{3,1,2,0:T(8,128)(2,1)S(1)} copy(bf16[2,64,2,2048]{3,2,1,0:T(2,128)(2,1)} %bitcast.25) | data formatting | bytes 2097152 | tf_op jit(solution)/shard_map/reshape | solution.py:347
  4.9 0.0 copy-done.4
  4.9 0.4 copy.17
  5.3 0.0 copy-done.3
  5.3 18.2 %shard_map.91 = (bf16[16,4,128,128]{3,2,1,0:T(8,128)(2,1)S(1)}, f32[16,2,128,128]{3,2,1,0:T(8,128)S(1)}) custom-call(bf16[256,2048]{1,0:T(8,128)(2,1)S(1)} %bitcast.21, bf16[256,2048]{1,0:T(8,128)(2,1)S(1)} %bitcast.22, bf16[128,2048]{1,0:T(8,128)(2,1)S(1)} %copy-done.3, f32[256,16]{1,0:T(8,128)S(1)} %bitcast.24, f32[128,16]{1,0:T(8,128)S(1)} %copy.21.ctok_ref, ...), custom_call_target="tpu_custom_call" | custom-call | tf_op jit(solution)/shard_map/pallas_call | solution.py:352
  23.5 0.0 copy-start.1
  23.5 1.3 %copy-done.1 = bf16[16,4,128,128]{3,2,1,0:T(8,128)(2,1)} copy-done((bf16[16,4,128,128]{3,2,1,0:T(8,128)(2,1)}, bf16[16,4,128,128]{3,2,1,0:T(8,128)(2,1)S(1)}, u32[]{:S(2)}) %copy-start.1) | copy-done | bytes 2097176
  24.8 0.0 copy-start.2
  24.8 1.3 %copy-done.2 = f32[16,2,128,128]{3,2,1,0:T(8,128)} copy-done((f32[16,2,128,128]{3,2,1,0:T(8,128)}, f32[16,2,128,128]{3,2,1,0:T(8,128)S(1)}, u32[]{:S(2)}) %copy-start.2) | copy-done | bytes 2097176
  26.1 59.7 %shard_map.92 = bf16[128,2048]{1,0:T(8,128)(2,1)} custom-call(bf16[16,4,128,128]{3,2,1,0:T(8,128)(2,1)} %copy-done.1, f32[16,2,128,128]{3,2,1,0:T(8,128)} %copy-done.2, bf16[128,2048]{1,0:T(8,128)(2,1)} %gate_ref.1, f32[16,1,128]{2,1,0:T(1,128)} %broadcast_in_dim.26.end_ref, f32[1,128]{1,0:T(1,128)} %bitcast.31, bf16[4096,2048]{1,0:T(8,128)(2,1)} %w_ref.1), custom_call_target="tpu_custom_call" | custom-call | tf_op jit(solution)/shard_map/pallas_call | solution.py:379
  85.8 1.9 %copy.27 = bf16[128,2048]{1,0:T(8,128)(2,1)} copy(bf16[128,2048]{1,0:T(8,128)(2,1)} %shard_map.92) | data formatting | bytes 1048576
  (3 shorter events, 0.1 us)
Async XLA Ops:
  0.0 0.8 copy-start
  0.0 4.9 %copy-start.4 = (bf16[128,2,2048]{2,1,0:T(2,128)(2,1)S(1)}, bf16[128,2,2048]{2,1,0:T(2,128)(2,1)}, u32[]{:S(2)}) copy-start(bf16[128,2,2048]{2,1,0:T(2,128)(2,1)} %param.11) | copy-start | bytes 3145732
  3.3 2.0 %copy-start.3 = (bf16[128,2048]{1,0:T(8,128)(2,1)S(1)}, bf16[128,2048]{1,0:T(8,128)(2,1)}, u32[]{:S(2)}) copy-start(bf16[128,2048]{1,0:T(8,128)(2,1)} %q_ref.1) | copy-start | bytes 1572868
  23.5 1.3 %copy-start.1 = (bf16[16,4,128,128]{3,2,1,0:T(8,128)(2,1)}, bf16[16,4,128,128]{3,2,1,0:T(8,128)(2,1)S(1)}, u32[]{:S(2)}) copy-start(bf16[16,4,128,128]{3,2,1,0:T(8,128)(2,1)S(1)} %get-tuple-element.7.map_hbm) | copy-start | bytes 6291460
  24.8 1.3 %copy-start.2 = (f32[16,2,128,128]{3,2,1,0:T(8,128)}, f32[16,2,128,128]{3,2,1,0:T(8,128)S(1)}, u32[]{:S(2)}) copy-start(f32[16,2,128,128]{3,2,1,0:T(8,128)S(1)} %get-tuple-element.8.add_hbm) | copy-start | bytes 6291460

commit v5 on v4

--- a/solution.py
+++ b/solution.py
@@ -159,6 +159,7 @@
     other = 1 - core
     part = DK // 2
     relays = (odd == 0) & (me < n - 2)
+    late = me >= n // 2
 
     def load_map(h):
         return pltpu.make_async_copy(map_hbm.at[h], maps.at[h], map_sem.at[h])
@@ -246,6 +247,17 @@
         ).astype(BF16)
         joint_add[h] = theirs_end * add + mm_t(add.astype(BF16), theirs) + mates[h, 1].astype(F32)
 
+    def project(base):
+        block = jnp.concatenate([gated[base + i] for i in range(group)], axis=1)
+        start = pl.multiple_of(base * DK, group * DK)
+        return mm(block, w_vmem[pl.ds(start, group * DK), :])
+
+    total[...] = jnp.zeros_like(total)
+
+    @pl.when(late)
+    def _():
+        load.wait()
+
     ready(0)
 
     @pl.when(odd == 0)
@@ -289,18 +301,17 @@
         gated[core * heads + h] = (rows * scale * gain_ref[...] * (x / (1.0 + jnp.exp(-x)))).astype(BF16)
         across(h).start()
 
-    load.wait()
-
-    def project(base):
-        block = jnp.concatenate([gated[base + i] for i in range(group)], axis=1)
-        start = pl.multiple_of(base * DK, group * DK)
-        return mm(block, w_vmem[pl.ds(start, group * DK), :])
-
-    total[...] = project(core * heads)
-
-    @pl.loop(1, heads // group)
-    def _(g):
-        total[...] += project(core * heads + g * group)
+        @pl.when(late & (lax.rem(h, group) == group - 1))
+        def _():
+            total[...] += project(core * heads + (h - (group - 1)))
+
+    @pl.when(jnp.logical_not(late))
+    def _():
+        load.wait()
+
+        @pl.loop(0, heads // group)
+        def _(g):
+            total[...] += project(core * heads + g * group)
 
     @pl.loop(0, heads // group)
     def _(g):

time: 88 us -> 87.4 us (level)
  no operation moved by 1% of the time
where the time goes in v5:
time: 87.4 us; the launch traced here: 87.2 us
  Pallas kernels  77.3 us (88%)
  local copies, waits for them, and re-layouts  8.13 us (9%)
  other arithmetic  1.47 us (2%)
    pallas_call x1, Pallas kernels, shards(): pl.pallas_call(functools.partial(relay_kernel, n, heads, group), in_specs...  59.2 us
    pallas_call x1, Pallas kernels, shards(): pl.pallas_call(functools.partial(prepare_kernel, together), grid=(heads /...  18.2 us
    unnamed x12, local copies, waits for them, and re-layouts  4.62 us

profile of v5, /device:TPU:30, one launch (start us, length us, event | category | flops | bytes accessed | tf_op | source)
XLA Modules:
  0.0 87.2 jit_solution(6681268529394234910)
XLA Ops:
  0.0 0.0 copy-start
  0.0 0.0 copy-start.4
  0.0 0.7 compare_convert_fusion
  0.8 0.0 copy-done
  0.8 0.1 fusion
  0.9 0.2 fusion.1
  1.1 0.7 broadcast_in_dim.26.end_ref
  1.8 0.7 broadcast_multiply_fusion
  2.5 0.1 reshape.49
  2.6 0.1 broadcast_in_dim.10
  2.7 0.1 broadcast_in_dim_reshape.6.cum_ref
  2.8 0.1 broadcast_in_dim_reshape.7.s_ref
  2.9 0.1 copy.23
  3.0 0.1 copy.21.ctok_ref
  3.1 0.1 copy.20
  3.3 0.0 copy-start.3
  3.3 1.6 %copy.16 = bf16[2,64,2,2048]{3,1,2,0:T(8,128)(2,1)S(1)} copy(bf16[2,64,2,2048]{3,2,1,0:T(2,128)(2,1)} %bitcast.25) | data formatting | bytes 2097152 | tf_op jit(solution)/shard_map/reshape | solution.py:358
  4.9 0.0 copy-done.4
  4.9 0.4 copy.17
  5.3 0.0 copy-done.3
  5.3 18.2 %shard_map.91 = (bf16[16,4,128,128]{3,2,1,0:T(8,128)(2,1)S(1)}, f32[16,2,128,128]{3,2,1,0:T(8,128)S(1)}) custom-call(bf16[256,2048]{1,0:T(8,128)(2,1)S(1)} %bitcast.21, bf16[256,2048]{1,0:T(8,128)(2,1)S(1)} %bitcast.22, bf16[128,2048]{1,0:T(8,128)(2,1)S(1)} %copy-done.3, f32[256,16]{1,0:T(8,128)S(1)} %bitcast.24, f32[128,16]{1,0:T(8,128)S(1)} %copy.21.ctok_ref, ...), custom_call_target="tpu_custom_call" | custom-call | tf_op jit(solution)/shard_map/pallas_call | solution.py:363
  23.5 0.0 copy-start.1
  23.5 1.3 %copy-done.1 = bf16[16,4,128,128]{3,2,1,0:T(8,128)(2,1)} copy-done((bf16[16,4,128,128]{3,2,1,0:T(8,128)(2,1)}, bf16[16,4,128,128]{3,2,1,0:T(8,128)(2,1)S(1)}, u32[]{:S(2)}) %copy-start.1) | copy-done | bytes 2097176
  24.8 0.0 copy-start.2
  24.8 1.3 %copy-done.2 = f32[16,2,128,128]{3,2,1,0:T(8,128)} copy-done((f32[16,2,128,128]{3,2,1,0:T(8,128)}, f32[16,2,128,128]{3,2,1,0:T(8,128)S(1)}, u32[]{:S(2)}) %copy-start.2) | copy-done | bytes 2097176
  26.1 59.2 %shard_map.92 = bf16[128,2048]{1,0:T(8,128)(2,1)} custom-call(bf16[16,4,128,128]{3,2,1,0:T(8,128)(2,1)} %copy-done.1, f32[16,2,128,128]{3,2,1,0:T(8,128)} %copy-done.2, bf16[128,2048]{1,0:T(8,128)(2,1)} %gate_ref.1, f32[16,1,128]{2,1,0:T(1,128)} %broadcast_in_dim.26.end_ref, f32[1,128]{1,0:T(1,128)} %bitcast.31, bf16[4096,2048]{1,0:T(8,128)(2,1)} %w_ref.1), custom_call_target="tpu_custom_call" | custom-call | tf_op jit(solution)/shard_map/pallas_call | solution.py:390
  85.3 1.9 %copy.27 = bf16[128,2048]{1,0:T(8,128)(2,1)} copy(bf16[128,2048]{1,0:T(8,128)(2,1)} %shard_map.92) | data formatting | bytes 1048576
  (3 shorter events, 0.1 us)
Async XLA Ops:
  0.0 0.8 copy-start
  0.0 4.9 %copy-start.4 = (bf16[128,2,2048]{2,1,0:T(2,128)(2,1)S(1)}, bf16[128,2,2048]{2,1,0:T(2,128)(2,1)}, u32[]{:S(2)}) copy-start(bf16[128,2,2048]{2,1,0:T(2,128)(2,1)} %param.11) | copy-start | bytes 3145732
  3.3 2.0 %copy-start.3 = (bf16[128,2048]{1,0:T(8,128)(2,1)S(1)}, bf16[128,2048]{1,0:T(8,128)(2,1)}, u32[]{:S(2)}) copy-start(bf16[128,2048]{1,0:T(8,128)(2,1)} %q_ref.1) | copy-start | bytes 1572868
  23.5 1.3 %copy-start.1 = (bf16[16,4,128,128]{3,2,1,0:T(8,128)(2,1)}, bf16[16,4,128,128]{3,2,1,0:T(8,128)(2,1)S(1)}, u32[]{:S(2)}) copy-start(bf16[16,4,128,128]{3,2,1,0:T(8,128)(2,1)S(1)} %get-tuple-element.7.map_hbm) | copy-start | bytes 6291460
  24.8 1.3 %copy-start.2 = (f32[16,2,128,128]{3,2,1,0:T(8,128)}, f32[16,2,128,128]{3,2,1,0:T(8,128)S(1)}, u32[]{:S(2)}) copy-start(f32[16,2,128,128]{3,2,1,0:T(8,128)S(1)} %get-tuple-element.8.add_hbm) | copy-start | bytes 6291460
